TPU v7x, 32 devices: a whole 2x2x4 slice. The times are simulated.
32 devices in a mesh: parts: 2 (over y), gy: 8 (over z, x), gz: 2 (over core).
Axes of the slice: x: 2, y: 2, z: 4, core: 2. Of those that a mesh axis runs over, the one named last changes fastest.
Arguments:
- volume: bfloat16 [32, 64, 4096], P(('parts', 'gz'), 'gy'), parts along dimension 0, may hold values from 0 to 1
- column_weight: float32 [8, 64], P('parts', 'gy'), parts along dimension 0, may hold values from 0.02 to 0.2
- tile_xblock: int32 [8, 8, 32, 6], P('parts', 'gy'), parts along dimension 0, may hold values from 0 to 31, as said below
- tile_bank: int32 [8, 8, 32, 6], P('parts', 'gy'), parts along dimension 0, may hold values from 0 to 15
- tile_count: int32 [8, 8, 32], P('parts', 'gy'), parts along dimension 0, may hold values from 1 to 6, as said below
- footprint: bfloat16 [16, 128, 128], replicated, may hold values from -0.375 to 0.375
- cone_extent: int32 [8, 4096], P('parts', 'gy'), parts along dimension 0, may hold values from 1 to 4
- measured: float32 [8, 16, 4096], P('parts', 'gz', 'gy'), parts along dimension 0, may hold values from -8 to 8
- ray_length: float32 [8, 16, 4096], P('parts', 'gz', 'gy'), parts along dimension 0, may hold values from 0.5 to 2
Outputs:
- new_volume: bfloat16 [32, 64, 4096], P(('parts', 'gz'), 'gy'), parts along dimension 0
- back_rows: float32 [8, 16, 4096], P('parts', 'gz', 'gy'), parts along dimension 0
There are 2 independent parts, one for each index of `parts`. A program takes and returns all parts, laid end to end along the dimension named above; an argument that names none is the same for every part. Nothing has to cross between parts.
Inputs may be any that keep to these rules, and one draw needn't show every extreme that they name: Slots s >= tile_count of a list hold valid entries that are not used; a list's used slots are most numerous at central y groups and central detector tiles. `tile_xblock`: an x tile index.
All inputs are finite; a program needn't handle non-finite values.
Results may differ from a plain program's by a relative error of at most 0.0052.
Values may be sent and summed in bfloat16 or wider, within the bound.
A program may use at most 64 MiB of HBM per device.

v0:
```python
import math

import jax
import jax.numpy as jnp
from jax import lax
from jax.sharding import PartitionSpec as P

SLOTS = 6
TILE = 128


CONE_WEIGHTS = (0.45, 0.3, 0.2, 0.12)


def extended(cells, sides, width):
    for axis, dim in sides:
        count = lax.axis_size(axis)
        ends = count - 1
        head = lax.slice_in_dim(cells, 0, width, axis=dim)
        tail = lax.slice_in_dim(cells, cells.shape[dim] - width, cells.shape[dim], axis=dim)
        cells = jnp.concatenate(
            [
                lax.ppermute(tail, axis, [(i, (i + 1) % count) for i in range(ends)]),
                cells,
                lax.ppermute(head, axis, [((i + 1) % count, i) for i in range(ends)]),
            ],
            axis=dim,
        )
    return cells


def cone(signal, extent):
    spread = len(CONE_WEIGHTS)
    depth = signal.shape[1]
    padded = extended(signal, (("gz", 1),), spread)
    summed = signal
    for offset in range(1, spread + 1):
        gating = (extent >= offset).astype(jnp.float32)[:, None, :]
        beside_all = (
            padded[:, spread - offset : spread - offset + depth]
            + padded[:, spread + offset : spread + offset + depth]
        )
        summed = summed + CONE_WEIGHTS[offset - 1] * gating * beside_all
    return summed


def weighted(columns, weights):
    return jnp.sum(columns.astype(jnp.float32) * weights[None, :, None], axis=1).astype(
        jnp.bfloat16
    )


def forward_part(rows_in, xblock, bank_ids, filled, footprint):
    depth = rows_in.shape[0]
    count_tiles = xblock.shape[0]
    blocks = rows_in.reshape(depth, count_tiles, TILE).transpose(1, 0, 2)
    per_map = math.gcd(count_tiles, 8)

    def forward_one_block(inputs):
        xpart, bpart, fpart = inputs
        usable = (jnp.arange(SLOTS)[None, :] < fpart[:, None]).astype(jnp.bfloat16)
        left_tiles = blocks[xpart] * usable[:, :, None, None]
        return jnp.einsum(
            "tszj,tsji->tzi", left_tiles, footprint[bpart], preferred_element_type=jnp.float32
        )

    result = lax.map(
        forward_one_block,
        (
            xblock.reshape(-1, per_map, SLOTS),
            bank_ids.reshape(-1, per_map, SLOTS),
            filled.reshape(-1, per_map),
        ),
    )
    return result.reshape(count_tiles, depth, TILE).transpose(1, 0, 2).reshape(depth, -1)


def back_part(sent_rows, xblock, bank_ids, filled, footprint):
    depth = sent_rows.shape[0]
    count_tiles = xblock.shape[0]
    blocks = sent_rows.reshape(depth, count_tiles, TILE).transpose(1, 0, 2)
    per_map = math.gcd(count_tiles, 8)

    def back_one_block(inputs):
        bpart, fpart, rpart = inputs
        usable = (jnp.arange(SLOTS)[None, :] < fpart[:, None]).astype(jnp.float32)
        products = jnp.einsum(
            "tzi,tsji->tszj", rpart, footprint[bpart], preferred_element_type=jnp.float32
        )
        return products * usable[:, :, None, None]

    spread_out = lax.map(
        back_one_block,
        (
            bank_ids.reshape(-1, per_map, SLOTS),
            filled.reshape(-1, per_map),
            blocks.reshape(-1, per_map, depth, TILE),
        ),
    )
    spread_out = spread_out.reshape(count_tiles * SLOTS, depth * TILE)
    summed = jnp.zeros((count_tiles, depth * TILE), jnp.float32)
    summed = summed.at[xblock.reshape(-1)].add(spread_out)
    return summed.reshape(count_tiles, depth, TILE).transpose(1, 0, 2).reshape(depth, -1)


def shards(
    volume,
    column_weight,
    tile_xblock,
    tile_bank,
    tile_count,
    footprint,
    cone_extent,
    measured,
    ray_length,
):
    depth, width_cols, total_x = volume.shape
    angles = column_weight.shape[0]

    def project(angle_no):
        rows_in = weighted(volume, column_weight[angle_no])
        return forward_part(
            rows_in,
            tile_xblock[angle_no, 0],
            tile_bank[angle_no, 0],
            tile_count[angle_no, 0],
            footprint,
        )

    change = jnp.zeros((depth, width_cols, total_x), jnp.float32)
    partial_value = jnp.stack([project(angle_no) for angle_no in range(angles)])
    owned = lax.psum_scatter(partial_value, "gy", scatter_dimension=2, tiled=True)
    predicted = cone(owned, cone_extent)
    back_rows = cone((measured - predicted) / ray_length, cone_extent)
    sent = lax.all_gather(back_rows.astype(jnp.bfloat16), "gy", axis=2, tiled=True)
    for angle_no in range(angles):
        sent_rows = sent[angle_no]
        change = (
            change
            + column_weight[angle_no][None, :, None]
            * back_part(
                sent_rows,
                tile_xblock[angle_no, 0],
                tile_bank[angle_no, 0],
                tile_count[angle_no, 0],
                footprint,
            )[:, None, :]
        )
    new_volume = jnp.maximum(volume.astype(jnp.float32) + change, 0.0).astype(jnp.bfloat16)
    return (new_volume, back_rows)


def solution(mesh):
    in_specs = (
        P(("parts", "gz"), "gy", None),
        P("parts", "gy"),
        P("parts", "gy", None, None),
        P("parts", "gy", None, None),
        P("parts", "gy", None),
        P(),
        P("parts", "gy"),
        P("parts", "gz", "gy"),
        P("parts", "gz", "gy"),
    )
    out_specs = (P(("parts", "gz"), "gy", None), P("parts", "gz", "gy"))
    return jax.shard_map(shards, mesh=mesh, in_specs=in_specs, out_specs=out_specs, check_vma=False)
```

profile of v0, /device:TPU:0, one launch (start us, length us, event | category | flops | bytes accessed | tf_op | source)
XLA Modules:
  0.0 230.0 jit_solution(1846637173715942479)
XLA Ops:
  7.2 0.8 slice_reduce_fusion.11
  8.0 0.8 slice_reduce_fusion.3
  8.9 0.8 slice_bitcast_fusion
  10.6 2.7 %fusion.48 = (bf16[8,4096]{1,0:T(8,128)(2,1)S(1)}, bf16[8,4096]{1,0:T(8,128)(2,1)S(1)}, bf16[8,4096]{1,0:T(8,128)(2,1)S(1)}, bf16[8,4096]{1,0:T(8,128)(2,1)S(1)}) fusion(bf16[8,8,4096]{2,1,0:T(8,128)(2,1)} %param.25, f32[8]{0:T(128)S(1)} %get-tuple-element.434, f32[8]{0:T(128)S(1)} %get-tuple-element.433, f32[8]{0:T(128)S(1)} %get-tuple-element.435, ...), kind=kLoop, calls=%fused_computation.117 | loop fusion | flops 2228224 | bytes 786560 | tf_op jit(solution)/shard_map/reduce_sum | solution.py:48
  13.3 13.4 %while.83 = (s32[]{:T(128)}, f32[4,8,8,128]{3,2,1,0:T(8,128)S(1)}, s32[4,8,6]{1,0,2:T(4,128)S(1)}, bf16[32,8,128]{2,1,0:T(8,128)(2,1)S(1)}, s32[4,8]{1,0:T(4,128...) while((s32[]{:T(128)}, f32[4,8,8,128]{3,2,1,0:T(8,128)S(1)}, ...), condition=%wide.region_11.12_spmd, body=%wide.region_10.11_spmd.sunk | while | flops 12634498 | bytes 5059881 | solution.py:67
  13.5 1.9 gather_fusion.6
  16.9 1.9 gather_fusion.6
  20.2 1.9 gather_fusion.6
  23.6 1.9 gather_fusion.6
  27.0 13.4 %while.82 = (s32[]{:T(128)}, f32[4,8,8,128]{3,2,1,0:T(8,128)S(1)}, s32[4,8,6]{1,0,2:T(4,128)S(1)}, bf16[32,8,128]{2,1,0:T(8,128)(2,1)S(1)}, s32[4,8]{1,0:T(4,128...) while((s32[]{:T(128)}, f32[4,8,8,128]{3,2,1,0:T(8,128)S(1)}, ...), condition=%wide.region_8.9_spmd, body=%wide.region_7.8_spmd.sunk | while | flops 12634498 | bytes 5059881 | solution.py:67
  27.2 1.9 gather_fusion.4
  30.6 1.9 gather_fusion.4
  33.9 1.9 gather_fusion.4
  37.3 1.9 gather_fusion.4
  40.7 13.4 %while.81 = (s32[]{:T(128)}, f32[4,8,8,128]{3,2,1,0:T(8,128)S(1)}, s32[4,8,6]{1,0,2:T(4,128)S(1)}, bf16[32,8,128]{2,1,0:T(8,128)(2,1)S(1)}, s32[4,8]{1,0:T(4,128...) while((s32[]{:T(128)}, f32[4,8,8,128]{3,2,1,0:T(8,128)S(1)}, ...), condition=%wide.region_5.6_spmd, body=%wide.region_4.5_spmd.sunk | while | flops 12634498 | bytes 5059881 | solution.py:67
  40.9 1.9 gather_fusion.2
  44.2 1.9 gather_fusion.2
  47.6 1.9 gather_fusion.2
  50.9 1.9 gather_fusion.2
  54.3 13.4 %while.80 = (s32[]{:T(128)}, f32[4,8,8,128]{3,2,1,0:T(8,128)S(1)}, s32[4,8,6]{1,0,2:T(4,128)S(1)}, bf16[32,8,128]{2,1,0:T(8,128)(2,1)S(1)}, s32[4,8]{1,0:T(4,128...) while((s32[]{:T(128)}, f32[4,8,8,128]{3,2,1,0:T(8,128)S(1)}, ...), condition=%wide.region_2.3_spmd, body=%wide.region_1.2_spmd.sunk | while | flops 12634498 | bytes 5059881 | solution.py:67
  54.5 1.9 gather_fusion
  57.9 1.9 gather_fusion
  61.2 1.9 gather_fusion
  64.6 1.9 gather_fusion
  67.8 0.8 pad_maximum_fusion
  69.5 64.3 %reduce-scatter.2.cloned.1.call-done = f32[4,8,512]{2,1,0:T(8,128)} async-done(((f32[4,8,4096]{2,1,0:T(8,128)}), f32[4,8,512]{2,1,0:T(8,128)}) %reduce-scatter.2.cloned.1.call-update) | async-done | bytes 65552 | tf_op jit(solution)/shard_map/reduce_scatter | solution.py:132
  133.8 0.9 fusion.108
  134.7 1.3 collective-permute-start
  136.0 1.3 collective-permute-start.1
  137.3 0.8 constant_dynamic-update-slice_fusion.1
  138.2 1.0 collective-permute-done.1
  139.2 1.1 fusion.88
  140.3 1.3 collective-permute-start.3
  141.6 3.0 %collective-permute-start.2 = (f32[4,4,512]{2,1,0:T(4,128)S(1)}, f32[4,4,512]{2,1,0:T(4,128)S(1)}, u32[]{:S(2)}, u32[]{:S(2)}) collective-permute-start(f32[4,4,512]{2,1,0:T(4,128)S(1)} %get-tuple-element.420), channel_id=1, source_target_pairs={{0,1},{2,3},{4,5},{6,7},{8,9},{10,11},{12,13},{14,15},{16,17},{18,... | collective-permute-start | bytes 98312 | tf_op jit(solution)/shard_map/ppermute | solution.py:23
  146.2 30.7 %all_gather.3 = bf16[4,8,4096]{2,1,0:T(8,128)(2,1)S(1)} all-gather(bf16[4,8,512]{2,1,0:T(8,128)(2,1)S(1)} %get-tuple-element.406), channel_id=1, replica_groups=mesh['parts'=2,'gy'=8,'gz'=2] {'gy'}, dimensions={2}, use_global_device_ids=true | all-gather | bytes 294912 | tf_op jit(solution)/shard_map/all_gather | solution.py:135
  177.7 6.6 %while.87 = (s32[]{:T(128)}, f32[4,8,6,8,128]{4,3,2,1,0:T(8,128)S(1)}, s32[4,8,6]{1,0,2:T(4,128)S(1)}, bf16[16,128,128]{2,1,0:T(8,128)(2,1)S(1)}, bf16[4,8,8,128...) while((s32[]{:T(128)}, f32[4,8,6,8,128]{4,3,2,1,0:T(8,128)S(1)}, s32[4,8,6]{1,0,2:T(4,128)S(1)}, ...), condition=%wide.region_23.24_spmd, body=%wide.region_22.23_spmd.sunk | while | flops 12633330 | bytes 4942717 | solution.py:92
  177.9 0.9 gather_fusion.11
  179.6 0.9 gather_fusion.11
  181.2 0.9 gather_fusion.11
  182.9 0.9 gather_fusion.11
  184.3 2.3 %scatter_custom_fusion.3 = f32[32,1024]{1,0:T(8,128)S(1)} fusion(s32[192]{0:T(256)S(1)} %bitcast.431, f32[24,8,8,128]{3,2,1,0:T(8,128)S(1)} %bitcast.408, f32[]{:T(128)} %constant.129.clone.1), kind=kCustom, calls=%fused_computation.123 | custom fusion | flops 196608 | bytes 917508 | tf_op jit(solution)/shard_map/scatter-add | solution.py:102
  186.8 6.6 %while.86 = (s32[]{:T(128)}, f32[4,8,6,8,128]{4,3,2,1,0:T(8,128)S(1)}, s32[4,8,6]{1,0,2:T(4,128)S(1)}, bf16[16,128,128]{2,1,0:T(8,128)(2,1)S(1)}, bf16[4,8,8,128...) while((s32[]{:T(128)}, f32[4,8,6,8,128]{4,3,2,1,0:T(8,128)S(1)}, s32[4,8,6]{1,0,2:T(4,128)S(1)}, ...), condition=%wide.region_20.21_spmd, body=%wide.region_19.20_spmd.sunk | while | flops 12633330 | bytes 4942717 | solution.py:92
  187.0 0.9 gather_fusion.10
  188.6 0.9 gather_fusion.10
  190.3 0.9 gather_fusion.10
  191.9 0.9 gather_fusion.10
  193.4 2.5 %scatter_custom_fusion.2 = f32[32,1024]{1,0:T(8,128)S(1)} fusion(s32[192]{0:T(256)S(1)} %bitcast.430, f32[24,8,8,128]{3,2,1,0:T(8,128)S(1)} %bitcast.409, f32[]{:T(128)} %constant.129.clone.1), kind=kCustom, calls=%fused_computation.126 | custom fusion | flops 196608 | bytes 917508 | tf_op jit(solution)/shard_map/scatter-add | solution.py:102
  196.6 6.6 %while.85 = (s32[]{:T(128)}, f32[4,8,6,8,128]{4,3,2,1,0:T(8,128)S(1)}, s32[4,8,6]{1,0,2:T(4,128)S(1)}, bf16[16,128,128]{2,1,0:T(8,128)(2,1)S(1)}, bf16[4,8,8,128...) while((s32[]{:T(128)}, f32[4,8,6,8,128]{4,3,2,1,0:T(8,128)S(1)}, s32[4,8,6]{1,0,2:T(4,128)S(1)}, ...), condition=%wide.region_17.18_spmd, body=%wide.region_16.17_spmd.sunk | while | flops 12633330 | bytes 4942717 | solution.py:92
  196.8 0.9 gather_fusion.9
  198.5 0.9 gather_fusion.9
  200.1 0.9 gather_fusion.9
  201.8 0.9 gather_fusion.9
  203.2 2.3 %scatter_custom_fusion.1 = f32[32,1024]{1,0:T(8,128)S(1)} fusion(s32[192]{0:T(256)S(1)} %bitcast.429, f32[24,8,8,128]{3,2,1,0:T(8,128)S(1)} %bitcast.410, f32[]{:T(128)} %constant.129.clone.1), kind=kCustom, calls=%fused_computation.129 | custom fusion | flops 196608 | bytes 917508 | tf_op jit(solution)/shard_map/scatter-add | solution.py:102
  206.3 12.1 %while.84 = (s32[]{:T(128)}, f32[4,8,6,8,128]{4,3,2,1,0:T(8,128)S(1)}, s32[4,8,6]{1,0,2:T(4,128)S(1)}, bf16[16,128,128]{2,1,0:T(8,128)(2,1)S(1)}, bf16[4,8,8,128...) while((s32[]{:T(128)}, f32[4,8,6,8,128]{4,3,2,1,0:T(8,128)S(1)}, s32[4,8,6]{1,0,2:T(4,128)S(1)}, ...), condition=%wide.region_14.15_spmd, body=%wide.region_13.14_spmd.sunk | while | flops 12633330 | bytes 4942717 | solution.py:92
  206.5 0.9 gather_fusion.8
  208.1 1.2 fusion.181
  209.6 0.9 gather_fusion.8
  211.2 1.2 fusion.181
  212.6 0.9 gather_fusion.8
  214.2 1.2 fusion.181
  215.6 0.9 gather_fusion.8
  217.2 1.2 fusion.181
  218.5 2.5 %scatter_custom_fusion = f32[32,1024]{1,0:T(8,128)S(1)} fusion(s32[192]{0:T(256)} %bitcast.428, f32[24,8,8,128]{3,2,1,0:T(8,128)S(1)} %bitcast.411, f32[]{:T(128)} %constant.129.clone.1), kind=kCustom, calls=%fused_computation.132 | custom fusion | flops 196608 | bytes 918016 | tf_op jit(solution)/shard_map/scatter-add | solution.py:102
  221.0 2.2 fusion.53
  (351 shorter events, 42.4 us)
Async XLA Ops:
  7.2 126.6 %reduce-scatter.2.cloned.1.call-start = ((), (), s32[]{:S(2)}) async-start(), calls=%async_computation.1 | async-start | bytes 589824 | tf_op jit(solution)/shard_map/reduce_scatter | solution.py:132
  9.8 3.5 %copy-start.6 = (f32[8]{0:T(128)}, f32[8]{0:T(128)S(1)}, u32[]{:S(2)}) copy-start(f32[8]{0:T(128)S(1)} %get-tuple-element.433) | copy-start | bytes 100
  9.8 3.5 %copy-start.7 = (f32[8]{0:T(128)}, f32[8]{0:T(128)S(1)}, u32[]{:S(2)}) copy-start(f32[8]{0:T(128)S(1)} %get-tuple-element.434) | copy-start | bytes 100
  9.8 3.6 %copy-start.5 = (f32[8]{0:T(128)}, f32[8]{0:T(128)S(1)}, u32[]{:S(2)}) copy-start(f32[8]{0:T(128)S(1)} %get-tuple-element.432) | copy-start | bytes 100
  9.8 3.6 %copy-start.8 = (f32[8]{0:T(128)}, f32[8]{0:T(128)S(1)}, u32[]{:S(2)}) copy-start(f32[8]{0:T(128)S(1)} %get-tuple-element.435) | copy-start | bytes 100
  67.7 67.0 %copy-start.9 = (s32[4,8]{1,0:T(4,128)}, s32[4,8]{1,0:T(4,128)S(1)}, u32[]{:S(2)}) copy-start(s32[4,8]{1,0:T(4,128)S(1)} %get-tuple-element.978) | copy-start | bytes 388
  67.7 1.7 copy-start.4
  67.7 71.4 %copy-start.2 = (f32[4,8,512]{2,1,0:T(8,128)S(1)}, f32[4,8,512]{2,1,0:T(8,128)}, u32[]{:S(2)}) copy-start(f32[4,8,512]{2,1,0:T(8,128)} %param.33) | copy-start | bytes 196612
  67.8 71.4 %copy-start.3 = (f32[4,8,512]{2,1,0:T(8,128)S(1)}, f32[4,8,512]{2,1,0:T(8,128)}, u32[]{:S(2)}) copy-start(f32[4,8,512]{2,1,0:T(8,128)} %param.32) | copy-start | bytes 196612
  68.6 109.1 %copy-start = (bf16[16,128,128]{2,1,0:T(8,128)(2,1)S(1)}, bf16[16,128,128]{2,1,0:T(8,128)(2,1)}, u32[]{:S(2)}) copy-start(bf16[16,128,128]{2,1,0:T(8,128)(2,1)} %get-tuple-element.956) | copy-start | bytes 1572868
  134.7 4.4 %collective-permute-start = (f32[4,4,512]{2,1,0:T(4,128)S(1)}, f32[4,4,512]{2,1,0:T(4,128)S(1)}, u32[]{:S(2)}, u32[]{:S(2)}) collective-permute-start(f32[4,4,512]{2,1,0:T(4,128)S(1)} %get-tuple-element.423), channel_id=1, source_target_pairs={{0,1},{2,3},{4,5},{6,7},{8,9},{10,11},{12,13},{14,15},{16,17},{18,... | collective-permute-start | bytes 98312 | tf_op jit(solution)/shard_map/ppermute | solution.py:23
  136.0 3.1 %collective-permute-start.1 = (f32[4,4,512]{2,1,0:T(4,128)S(1)}, f32[4,4,512]{2,1,0:T(4,128)S(1)}, u32[]{:S(2)}, u32[]{:S(2)}) collective-permute-start(f32[4,4,512]{2,1,0:T(4,128)S(1)} %get-tuple-element.422), channel_id=1, source_target_pairs={{1,0},{3,2},{5,4},{7,6},{9,8},{11,10},{13,12},{15,14},{17,16},{19,... | collective-permute-start | bytes 98312 | tf_op jit(solution)/shard_map/ppermute | solution.py:25
  140.3 4.9 %collective-permute-start.3 = (f32[4,4,512]{2,1,0:T(4,128)S(1)}, f32[4,4,512]{2,1,0:T(4,128)S(1)}, u32[]{:S(2)}, u32[]{:S(2)}) collective-permute-start(f32[4,4,512]{2,1,0:T(4,128)S(1)} %get-tuple-element.421), channel_id=1, source_target_pairs={{1,0},{3,2},{5,4},{7,6},{9,8},{11,10},{13,12},{15,14},{17,16},{19,... | collective-permute-start | bytes 98312 | tf_op jit(solution)/shard_map/ppermute | solution.py:25
  141.6 3.9 %collective-permute-start.2 = (f32[4,4,512]{2,1,0:T(4,128)S(1)}, f32[4,4,512]{2,1,0:T(4,128)S(1)}, u32[]{:S(2)}, u32[]{:S(2)}) collective-permute-start(f32[4,4,512]{2,1,0:T(4,128)S(1)} %get-tuple-element.420), channel_id=1, source_target_pairs={{0,1},{2,3},{4,5},{6,7},{8,9},{10,11},{12,13},{14,15},{16,17},{18,... | collective-permute-start | bytes 98312 | tf_op jit(solution)/shard_map/ppermute | solution.py:23
  206.3 14.6 %copy-start.1 = (bf16[8,8,4096]{2,1,0:T(8,128)(2,1)S(1)}, bf16[8,8,4096]{2,1,0:T(8,128)(2,1)}, u32[]{:S(2)}) copy-start(bf16[8,8,4096]{2,1,0:T(8,128)(2,1)} %param.25) | copy-start | bytes 1572868
Sparse Core Ops, SparseCore 0:
  68.7 64.9 reduce-scatter.1
where the time goes:
time: 232 us; the launch traced here: 230 us
  local copies, waits for them, and re-layouts  73.5 us (32%)
  waiting for transfers between devices  65.5 us (28%)
  blocking collectives  30.7 us (13%)
  other arithmetic  21.3 us (9%)
  matrix products  16.7 us (7%)
  between operations  14.4 us (6%)
  starting transfers between devices  6.94 us (3%)
    reduce_scatter x1, waiting for transfers between devices, shards(): lax.psum_scatter(partial_value, 'gy', scatter_dimension=2, tiled=True)  64.3 us
    all_gather x1, blocking collectives, shards(): lax.all_gather(back_rows.astype(jnp.bfloat16), 'gy', axis=2, tiled=True)  30.7 us
    gather x16, local copies, waits for them, and re-layouts, forward_one_block(): footprint[bpart]  30.3 us
    gather x16, local copies, waits for them, and re-layouts, back_one_block(): footprint[bpart]  13.6 us
    dot_general x16, matrix products, back_one_block(): jnp.einsum('tzi,tsji->tszj', rpart, footprint[bpart], preferred_element_t...  10.9 us
    gather x16, local copies, waits for them, and re-layouts, forward_one_block(): left_tiles = blocks[xpart] * usable[:, :, None, None]  9.78 us
    scatter-add x4, other arithmetic, back_part(): summed = summed.at[xblock.reshape(-1)].add(spread_out)  9.6 us
    dot_general x16, matrix products, forward_one_block(): jnp.einsum('tszj,tsji->tzi', left_tiles, footprint[bpart], preferred_elem...  5.82 us
  transfers between devices with their start and end apart: 5, of which 3 were waited for; matrix products, arithmetic and copies ran while one was open for 1% of the time, Pallas kernels for 0%

commit v1 on v0

v1 whole, which is shorter than its diff:
```python
import functools

import jax
import jax.numpy as jnp
from jax import lax
from jax.experimental import pallas as pl
from jax.experimental.pallas import tpu as pltpu
from jax.sharding import PartitionSpec as P

TILE = 128
ROWS = 8
CONE_WEIGHTS = (0.45, 0.3, 0.2, 0.12)
VMEM_LIMIT = 48 * 2**20
MESH = pl.DeviceIdType.MESH


def extended(cells, axis, dim, width):
    count = lax.axis_size(axis)
    ends = count - 1
    head = lax.slice_in_dim(cells, 0, width, axis=dim)
    tail = lax.slice_in_dim(cells, cells.shape[dim] - width, cells.shape[dim], axis=dim)
    return jnp.concatenate(
        [
            lax.ppermute(tail, axis, [(i, (i + 1) % count) for i in range(ends)]),
            cells,
            lax.ppermute(head, axis, [((i + 1) % count, i) for i in range(ends)]),
        ],
        axis=dim,
    )


def cone_across(signal, extent):
    spread = len(CONE_WEIGHTS)
    depth = signal.shape[1]
    padded = extended(signal, "gz", 1, spread)
    summed = signal
    for offset in range(1, spread + 1):
        gating = (extent >= offset).astype(jnp.float32)[:, None, :]
        beside = (
            padded[:, spread - offset : spread - offset + depth]
            + padded[:, spread + offset : spread + offset + depth]
        )
        summed = summed + CONE_WEIGHTS[offset - 1] * gating * beside
    return summed


def weight_matrix(w_ref, shape, angle_z, z_col):
    angles, cols = w_ref.shape
    a, z = angle_z
    zz, c = z_col
    key = a * cols + c
    out = jnp.zeros(shape, jnp.float32)
    for an in range(angles):
        for cn in range(cols):
            out = jnp.where(key == an * cols + cn, w_ref[an, cn], out)
    return jnp.where(z == zz, out, 0.0)


def split_part(value, part):
    high = value.astype(jnp.bfloat16).astype(jnp.float32)
    rest = value - high
    mid = rest.astype(jnp.bfloat16).astype(jnp.float32)
    return jnp.where(part == 0, high, jnp.where(part == 1, mid, rest - mid)).astype(jnp.bfloat16)


def column_sums(w_ref, vol_ref, lhs_ref):
    angles, cols = w_ref.shape
    depth, _, total = vol_ref.shape
    m = angles * depth
    shape = (3 * m, depth * cols)
    row = lax.broadcasted_iota(jnp.int32, shape, 0)
    col = lax.broadcasted_iota(jnp.int32, shape, 1)
    zb = depth.bit_length() - 1
    cb = cols.bit_length() - 1
    inner = row & (m - 1)
    w = weight_matrix(
        w_ref, shape, (inner >> zb, inner & (depth - 1)), (col >> cb, col & (cols - 1))
    )
    w3 = split_part(w, row >> (m.bit_length() - 1))
    step = 4 * TILE

    def body(i, carry):
        at = pl.ds(pl.multiple_of(i * step, step), step)
        v = jnp.concatenate([vol_ref[z, :, at].astype(jnp.float32) for z in range(depth)], axis=0)
        r = jnp.dot(w3, v.astype(jnp.bfloat16), preferred_element_type=jnp.float32)
        r = (r[:m] + (r[m : 2 * m] + r[2 * m :])).astype(jnp.bfloat16)
        for k in range(4):
            lhs_ref[pl.ds(pl.multiple_of((i * 4 + k) * m, m), m), :] = r[:, k * TILE : (k + 1) * TILE]
        return carry

    lax.fori_loop(0, total // step, body, 0)


def all_products(lhs_ref, fp_ref, prod_ref, transposed):
    banks = fp_ref.shape[0]
    total = lhs_ref.shape[0]
    blocks = total // ROWS
    chunk = 256
    prod_ref[pl.ds(banks * blocks, blocks)] = jnp.zeros((blocks, ROWS, TILE), jnp.float32)

    def body(i, carry):
        b = 2 * i
        if transposed:
            f = jnp.concatenate([fp_ref[b], fp_ref[b + 1]], axis=0)
            dims = (((1,), (1,)), ((), ()))
        else:
            f = jnp.concatenate([fp_ref[b], fp_ref[b + 1]], axis=1)
            dims = (((1,), (0,)), ((), ()))
        for k in range(total // chunk):
            p = lax.dot_general(
                lhs_ref[k * chunk : (k + 1) * chunk, :], f, dims, preferred_element_type=jnp.float32
            )
            n = chunk // ROWS
            for h in range(2):
                prod_ref[pl.ds((b + h) * blocks + k * n, n)] = p[
                    :, h * TILE : (h + 1) * TILE
                ].reshape(n, ROWS, TILE)
        return carry

    lax.fori_loop(0, banks // 2, body, 0)


def ray_sum(idx_ref, prod_ref, t, angles, tiles, slots):
    parts = []
    for a in range(angles):
        at = (a * tiles + t) * slots
        terms = [prod_ref[idx_ref[at + s]] for s in range(slots)]
        while len(terms) > 1:
            terms = [sum(terms[i : i + 2][1:], terms[i]) for i in range(0, len(terms), 2)]
        parts.append(terms[0])
    return jnp.concatenate(parts, axis=0)


def packed_slots(xblock, bank, count, banks):
    angles, _, tiles, slots = xblock.shape
    used = jnp.arange(slots)[None, None, :] < count[:, 0, :, None]
    b = jnp.where(used, bank[:, 0], banks)
    angle = jnp.arange(angles, dtype=jnp.int32)[:, None, None]
    return (b * (tiles * angles) + xblock[:, 0] * angles + angle).reshape(-1)


def back_kernel(idx_ref, w_ref, sent_ref, fp_ref, vol_ref, out_ref, lhs_ref, prod_ref, *acc_refs):
    angles, cols = w_ref.shape
    depth, _, total = vol_ref.shape
    tiles = total // TILE
    slots = idx_ref.shape[0] // (angles * tiles)
    m = angles * depth
    per = sent_ref.shape[2] // TILE
    for t in range(tiles):
        lhs_ref[t * m : (t + 1) * m, :] = sent_ref[t // per, :, (t % per) * TILE : (t % per + 1) * TILE]
    all_products(lhs_ref, fp_ref, prod_ref, True)
    for acc in acc_refs:
        acc[...] = jnp.zeros_like(acc)
    mask = tiles * angles - 1

    def body(t, carry):
        for s in range(slots):
            for a in range(angles):
                packed = idx_ref[(a * tiles + t) * slots + s]
                low = packed & mask
                x = low >> (angles.bit_length() - 1)
                acc_refs[a][x] += prod_ref[packed - low + (t * angles + a)]
        return carry

    lax.fori_loop(0, tiles, body, 0)

    shape = (depth * cols, 3 * m)
    row = lax.broadcasted_iota(jnp.int32, shape, 0)
    col = lax.broadcasted_iota(jnp.int32, shape, 1)
    zb = depth.bit_length() - 1
    cb = cols.bit_length() - 1
    inner = col & (m - 1)
    for extra in (1, 2):
        inner = jnp.where(col >= extra * m, (col - extra * m) & (m - 1), inner)
    w = weight_matrix(
        w_ref, shape, (inner >> zb, inner & (depth - 1)), (row >> cb, row & (cols - 1))
    )
    w3 = split_part(w, jnp.where(col >= 2 * m, 1, 0))
    step = 4

    def finish(i, carry):
        s = jnp.concatenate(
            [
                jnp.concatenate([acc_refs[a][i * step + k] for k in range(step)], axis=1)
                for a in range(angles)
            ],
            axis=0,
        )
        high = s.astype(jnp.bfloat16)
        low = (s - high.astype(jnp.float32)).astype(jnp.bfloat16)
        change = jnp.dot(
            w3, jnp.concatenate([high, low, high], axis=0), preferred_element_type=jnp.float32
        )
        at = pl.ds(pl.multiple_of(i * step * TILE, step * TILE), step * TILE)
        for z in range(depth):
            fresh = vol_ref[z, :, at].astype(jnp.float32) + change[z * cols : (z + 1) * cols]
            out_ref[z, :, at] = jnp.maximum(fresh, 0.0).astype(jnp.bfloat16)
        return carry

    lax.fori_loop(0, tiles // step, finish, 0)


SMEM = pl.BlockSpec(memory_space=pltpu.SMEM)
VMEM = pl.BlockSpec(memory_space=pltpu.VMEM)


def back(packed, column_weight, sent, footprint, volume):
    angles = column_weight.shape[0]
    depth, _, total = volume.shape
    tiles = total // TILE
    banks = footprint.shape[0]
    rows = tiles * angles * depth
    return pl.pallas_call(
        back_kernel,
        out_shape=jax.ShapeDtypeStruct(volume.shape, jnp.bfloat16),
        in_specs=[SMEM, SMEM, VMEM, VMEM, VMEM],
        out_specs=VMEM,
        scratch_shapes=[
            pltpu.VMEM((rows, TILE), jnp.bfloat16),
            pltpu.VMEM(((banks + 1) * tiles * angles, ROWS, TILE), jnp.float32),
        ]
        + [pltpu.VMEM((tiles, ROWS, TILE), jnp.float32) for _ in range(angles)],
        compiler_params=pltpu.CompilerParams(vmem_limit_bytes=VMEM_LIMIT),
        name="back_spread",
    )(packed, column_weight, sent, footprint, volume)


def forward_kernel(idx_ref, w_ref, fp_ref, vol_ref, out_ref, lhs_ref, prod_ref):
    angles = w_ref.shape[0]
    tiles = vol_ref.shape[2] // TILE
    slots = idx_ref.shape[0] // (angles * tiles)
    column_sums(w_ref, vol_ref, lhs_ref)
    all_products(lhs_ref, fp_ref, prod_ref, False)

    def body(t, carry):
        out_ref[:, pl.ds(pl.multiple_of(t * TILE, TILE), TILE)] = ray_sum(
            idx_ref, prod_ref, t, angles, tiles, slots
        )
        return carry

    lax.fori_loop(0, tiles, body, 0)


def forward(packed, column_weight, footprint, volume):
    angles = column_weight.shape[0]
    depth, _, total = volume.shape
    tiles = total // TILE
    banks = footprint.shape[0]
    rows = tiles * angles * depth
    return pl.pallas_call(
        forward_kernel,
        out_shape=jax.ShapeDtypeStruct((angles * depth, total), jnp.float32),
        in_specs=[SMEM, SMEM, VMEM, VMEM],
        out_specs=VMEM,
        scratch_shapes=[
            pltpu.VMEM((rows, TILE), jnp.bfloat16),
            pltpu.VMEM(((banks + 1) * tiles * angles, ROWS, TILE), jnp.float32),
        ],
        compiler_params=pltpu.CompilerParams(vmem_limit_bytes=VMEM_LIMIT),
        name="ray_sums",
    )(packed, column_weight, footprint, volume)


def shards(
    volume,
    column_weight,
    tile_xblock,
    tile_bank,
    tile_count,
    footprint,
    cone_extent,
    measured,
    ray_length,
):
    angles = column_weight.shape[0]
    depth, _, total = volume.shape
    packed = packed_slots(tile_xblock, tile_bank, tile_count, footprint.shape[0])
    partial = forward(packed, column_weight, footprint, volume).reshape(angles, depth, total)
    owned = lax.psum_scatter(partial, "gy", scatter_dimension=2, tiled=True)
    predicted = cone_across(owned, cone_extent)
    back_rows = cone_across((measured - predicted) / ray_length, cone_extent)
    sent = lax.all_gather(back_rows.astype(jnp.bfloat16), "gy", axis=2, tiled=True)
    new_volume = back(
        packed, column_weight, sent.reshape(1, angles * depth, total), footprint, volume
    )
    return new_volume, back_rows


def solution(mesh):
    in_specs = (
        P(("parts", "gz"), "gy", None),
        P("parts", "gy"),
        P("parts", "gy", None, None),
        P("parts", "gy", None, None),
        P("parts", "gy", None),
        P(),
        P("parts", "gy"),
        P("parts", "gz", "gy"),
        P("parts", "gz", "gy"),
    )
    out_specs = (P(("parts", "gz"), "gy", None), P("parts", "gz", "gy"))
    return jax.shard_map(shards, mesh=mesh, in_specs=in_specs, out_specs=out_specs, check_vma=False)
```

time: 232 us -> 142 us (0.61)
  local copies, waits for them, and re-layouts: 73.5 us -> 5.81 us
  other arithmetic: 21.3 us -> 1.67 us
  matrix products: 16.7 us -> 0 us
  Pallas kernels: 0 us -> 13.6 us
    gather x48 -> x0, local copies, waits for them, and re-layouts: 53.7 us -> none  [the longest x16 30.3 us: forward_one_block(): footprint[bpart]]
    dot_general x32 -> x0, matrix products: 16.7 us -> none  [the longest x16 10.9 us: back_one_block(): jnp.einsum('tzi,tsji->tszj', rpart, footprint[bpart], preferred_element_t...]
    pallas_call x0 -> x2, Pallas kernels: none -> 13.6 us  [the longest x1 7.44 us: back(): pl.pallas_call(back_kernel, out_shape=jax.ShapeDtypeStruct(volume.shape,...]
    scatter-add x4 -> x0, other arithmetic: 9.6 us -> none  [back_part(): summed = summed.at[xblock.reshape(-1)].add(spread_out)]
    select_n x96 -> x0, local copies, waits for them, and re-layouts: 7.83 us -> none  [the longest x32 2.61 us: forward_one_block(): footprint[bpart]]
    convert_element_type x33 -> x0, other arithmetic: 4.5 us -> none  [the longest x1 2.21 us: shards(): jnp.maximum(volume.astype(jnp.float32) + change, 0.0).astype(jnp.bfloat16)]
    slice x8 -> x0, local copies, waits for them, and re-layouts: 3.27 us -> none  [the longest x2 0.86 us: shards(): tile_xblock[angle_no, 0]]
    lt x32 -> x1, local copies, waits for them, and re-layouts: 2.98 us -> 0.15 us  [packed_slots(): used = jnp.arange(slots)[None, None, :] < count[:, 0, :, None]]
  transfers between devices with their start and end apart: 5 -> 5, of which waited for: 3 -> 3; matrix products, arithmetic and copies ran while one was open for 1% -> 0% of each run, Pallas kernels for 0% -> 0%
where the time goes in v1:
time: 142 us; the launch traced here: 141 us
  waiting for transfers between devices  67 us (47%)
  blocking collectives  30.7 us (22%)
  between operations  14.2 us (10%)
  Pallas kernels  13.6 us (10%)
  starting transfers between devices  8 us (6%)
  local copies, waits for them, and re-layouts  5.81 us (4%)
  other arithmetic  1.67 us (1%)
    reduce_scatter x1, waiting for transfers between devices, shards(): owned = lax.psum_scatter(partial, 'gy', scatter_dimension=2, tiled=True)  64.4 us
    all_gather x1, blocking collectives, shards(): lax.all_gather(back_rows.astype(jnp.bfloat16), 'gy', axis=2, tiled=True)  30.7 us
    pallas_call x1, Pallas kernels, back(): pl.pallas_call(back_kernel, out_shape=jax.ShapeDtypeStruct(volume.shape,...  7.44 us
    pallas_call x1, Pallas kernels, forward(): pl.pallas_call(forward_kernel, out_shape=jax.ShapeDtypeStruct((angles * d...  6.13 us
    ppermute x2, starting transfers between devices, extended(): lax.ppermute(tail, axis, [(i, (i + 1) % count) for i in range(ends)])  5.38 us
    unnamed x24, local copies, waits for them, and re-layouts  4.17 us
  transfers between devices with their start and end apart: 5, of which 3 were waited for; matrix products, arithmetic and copies ran while one was open for 0% of the time, Pallas kernels for 0%

profile of v1, /device:TPU:0, one launch (start us, length us, event | category | flops | bytes accessed | tf_op | source)
XLA Modules:
  0.0 141.0 jit_solution(16938492448016023707)
XLA Ops:
  7.2 0.0 reduce-scatter.2.cloned.1.call-start
  7.2 0.0 copy-start.10
  7.2 0.7 broadcast_multiply_fusion
  7.9 0.0 copy-done.10
  8.0 0.1 iota_compare_fusion
  8.0 0.1 lt.23
  8.2 0.1 copy.12
  8.3 0.0 copy-start.8
  8.3 0.1 mul.97
  8.4 0.6 copy-done.8
  9.0 0.1 copy.11
  9.1 0.1 squeeze.4
  9.3 0.1 add.67
  9.4 0.0 copy-start.4
  9.4 0.7 copy-done.4
  10.1 0.0 copy-start
  10.1 1.0 copy-done
  11.1 0.0 copy-start.2
  11.1 1.0 copy-done.2
  12.2 6.1 %ray_sums.1 = f32[32,4096]{1,0:T(8,128)} custom-call(s32[768]{0:T(1024)S(1)} %add_add_fusion.idx_ref, f32[4,8]{1,0:T(4,128)S(1)} %copy-done.4, bf16[16,128,128]{2,1,0:T(8,128)(2,1)S(1)} %copy-done, bf16[8,8,4096]{2,1,0:T(8,128)(2,1)S(1)} %copy-done.2), custom_call_target="tpu_custom_call" | custom-call | tf_op jit(solution)/shard_map/ray_sums/pallas_call | solution.py:250
  18.3 0.0 copy-start.9
  18.3 0.0 reduce-scatter.2.cloned.1.call-update
  18.3 0.7 copy-done.9
  19.0 64.4 %reduce-scatter.2.cloned.1.call-done = f32[4,8,512]{2,1,0:T(8,128)} async-done(((f32[4,8,4096]{2,1,0:T(8,128)}), f32[4,8,512]{2,1,0:T(8,128)}) %reduce-scatter.2.cloned.1.call-update) | async-done | bytes 65552 | tf_op jit(solution)/shard_map/reduce_scatter | solution.py:279
  83.4 0.0 copy-start.5
  83.4 1.0 fusion.37
  84.4 1.3 collective-permute-start.1
  85.7 3.0 %collective-permute-start = (f32[4,4,512]{2,1,0:T(4,128)S(1)}, f32[4,4,512]{2,1,0:T(4,128)S(1)}, u32[]{:S(2)}, u32[]{:S(2)}) collective-permute-start(f32[4,4,512]{2,1,0:T(4,128)S(1)} %get-tuple-element.7), channel_id=1, source_target_pairs={{0,1},{2,3},{4,5},{6,7},{8,9},{10,11},{12,13},{14,15},{16,17},{18,... | collective-permute-start | bytes 98312 | tf_op jit(solution)/shard_map/ppermute | solution.py:24
  88.7 0.0 copy-done.5
  88.8 0.0 copy-start.7
  88.8 0.0 copy-start.6
  88.8 0.0 collective-permute-done.1
  88.8 0.8 collective-permute-done
  89.6 0.0 copy-done.7
  89.6 0.0 copy-done.6
  89.6 0.0 copy-start.1
  89.6 0.0 copy-start.3
  89.6 0.1 fusion.22
  89.8 2.3 %collective-permute-start.2 = (f32[4,4,512]{2,1,0:T(4,128)S(1)}, f32[4,4,512]{2,1,0:T(4,128)S(1)}, u32[]{:S(2)}, u32[]{:S(2)}) collective-permute-start(f32[4,4,512]{2,1,0:T(4,128)S(1)} %get-tuple-element.4), channel_id=1, source_target_pairs={{0,1},{2,3},{4,5},{6,7},{8,9},{10,11},{12,13},{14,15},{16,17},{18,... | collective-permute-start | bytes 98312 | tf_op jit(solution)/shard_map/ppermute | solution.py:24
  92.1 1.3 collective-permute-start.3
  93.4 0.0 collective-permute-done.2
  93.4 1.8 %collective-permute-done.3 = f32[4,4,512]{2,1,0:T(4,128)S(1)} collective-permute-done((f32[4,4,512]{2,1,0:T(4,128)S(1)}, f32[4,4,512]{2,1,0:T(4,128)S(1)}, u32[]{:S(2)}, u32[]{:S(2)}) %collective-permute-start.3) | collective-permute-done | bytes 32800 | tf_op jit(solution)/shard_map/ppermute | solution.py:26
  95.2 0.7 fusion.34
  96.0 30.7 %all_gather.3 = bf16[4,8,4096]{2,1,0:T(8,128)(2,1)S(1)} all-gather(bf16[4,8,512]{2,1,0:T(8,128)(2,1)S(1)} %get-tuple-element.2), channel_id=1, replica_groups=mesh['parts'=2,'gy'=8,'gz'=2] {'gy'}, dimensions={2}, use_global_device_ids=true | all-gather | bytes 294912 | tf_op jit(solution)/shard_map/all_gather | solution.py:282
  126.7 0.0 copy-done.1
  126.7 0.0 copy-done.3
  126.7 7.4 %back_spread.1 = bf16[8,8,4096]{2,1,0:T(8,128)(2,1)} custom-call(s32[768]{0:T(1024)S(1)} %add_add_fusion.idx_ref, f32[4,8]{1,0:T(4,128)S(1)} %copy-done.4, bf16[1,32,4096]{2,1,0:T(8,128)(2,1)S(1)} %bitcast.11, bf16[16,128,128]{2,1,0:T(8,128)(2,1)S(1)} %copy-done.1, bf16[8,8,4096]{2,1,0:T(8,128)(2,1)S(1)} %copy-done.3), custom_call_target="tpu_custom_call" | custom-call | tf_op jit(solution)/shard_map/back_spread/pallas_call | solution.py:213
  (6 shorter events, 0.1 us)
Async XLA Ops:
  7.2 76.3 %reduce-scatter.2.cloned.1.call-start = ((), (), s32[]{:S(2)}) async-start(), calls=%async_computation.1 | async-start | bytes 589824 | tf_op jit(solution)/shard_map/reduce_scatter | solution.py:279
  7.2 0.7 copy-start.10
  8.3 0.7 copy-start.8
  9.4 0.7 copy-start.4
  10.1 1.0 copy-start
  11.1 1.0 copy-start.2
  18.3 0.7 copy-start.9
  83.4 5.3 %copy-start.5 = (f32[4,8,512]{2,1,0:T(8,128)S(1)}, f32[4,8,512]{2,1,0:T(8,128)}, u32[]{:S(2)}) copy-start(f32[4,8,512]{2,1,0:T(8,128)} %reduce-scatter.2.cloned.1.call-done) | copy-start | bytes 196612
  84.4 4.4 %collective-permute-start.1 = (f32[4,4,512]{2,1,0:T(4,128)S(1)}, f32[4,4,512]{2,1,0:T(4,128)S(1)}, u32[]{:S(2)}, u32[]{:S(2)}) collective-permute-start(f32[4,4,512]{2,1,0:T(4,128)S(1)} %get-tuple-element.6), channel_id=1, source_target_pairs={{1,0},{3,2},{5,4},{7,6},{9,8},{11,10},{13,12},{15,14},{17,16},{19,... | collective-permute-start | bytes 98312 | tf_op jit(solution)/shard_map/ppermute | solution.py:26
  85.7 3.9 %collective-permute-start = (f32[4,4,512]{2,1,0:T(4,128)S(1)}, f32[4,4,512]{2,1,0:T(4,128)S(1)}, u32[]{:S(2)}, u32[]{:S(2)}) collective-permute-start(f32[4,4,512]{2,1,0:T(4,128)S(1)} %get-tuple-element.7), channel_id=1, source_target_pairs={{0,1},{2,3},{4,5},{6,7},{8,9},{10,11},{12,13},{14,15},{16,17},{18,... | collective-permute-start | bytes 98312 | tf_op jit(solution)/shard_map/ppermute | solution.py:24
  88.8 0.8 copy-start.7
  88.8 0.9 copy-start.6
  89.6 37.1 %copy-start.1 = (bf16[16,128,128]{2,1,0:T(8,128)(2,1)S(1)}, bf16[16,128,128]{2,1,0:T(8,128)(2,1)}, u32[]{:S(2)}) copy-start(bf16[16,128,128]{2,1,0:T(8,128)(2,1)} %fp_ref.3) | copy-start | bytes 1572868
  89.6 37.1 %copy-start.3 = (bf16[8,8,4096]{2,1,0:T(8,128)(2,1)S(1)}, bf16[8,8,4096]{2,1,0:T(8,128)(2,1)}, u32[]{:S(2)}) copy-start(bf16[8,8,4096]{2,1,0:T(8,128)(2,1)} %vol_ref.3) | copy-start | bytes 1572868
  89.8 3.7 %collective-permute-start.2 = (f32[4,4,512]{2,1,0:T(4,128)S(1)}, f32[4,4,512]{2,1,0:T(4,128)S(1)}, u32[]{:S(2)}, u32[]{:S(2)}) collective-permute-start(f32[4,4,512]{2,1,0:T(4,128)S(1)} %get-tuple-element.4), channel_id=1, source_target_pairs={{0,1},{2,3},{4,5},{6,7},{8,9},{10,11},{12,13},{14,15},{16,17},{18,... | collective-permute-start | bytes 98312 | tf_op jit(solution)/shard_map/ppermute | solution.py:24
  92.1 3.1 %collective-permute-start.3 = (f32[4,4,512]{2,1,0:T(4,128)S(1)}, f32[4,4,512]{2,1,0:T(4,128)S(1)}, u32[]{:S(2)}, u32[]{:S(2)}) collective-permute-start(f32[4,4,512]{2,1,0:T(4,128)S(1)} %get-tuple-element.5), channel_id=1, source_target_pairs={{1,0},{3,2},{5,4},{7,6},{9,8},{11,10},{13,12},{15,14},{17,16},{19,... | collective-permute-start | bytes 98312 | tf_op jit(solution)/shard_map/ppermute | solution.py:26
Sparse Core Ops, SparseCore 0:
  18.5 64.9 reduce-scatter.1

commit v2 on v1

--- a/solution.py
+++ b/solution.py
@@ -261,6 +261,225 @@
     )(packed, column_weight, footprint, volume)
 
 
+def cone_rows(f, gates):
+    depth, width = f.shape
+    summed = f
+    for h, gate in enumerate(gates, 1):
+        zero = jnp.zeros((h, width), jnp.float32)
+        beside = jnp.concatenate([zero, f[: depth - h]], axis=0) + jnp.concatenate(
+            [f[h:], zero], axis=0
+        )
+        summed = summed + gate * beside
+    return summed
+
+
+def exchange_kernel(
+    count,
+    idx_ref,
+    w_ref,
+    fp_ref,
+    vol_ref,
+    ext_ref,
+    meas_ref,
+    ray_ref,
+    back_ref,
+    sent_ref,
+    lhs_ref,
+    prod_ref,
+    out_buf,
+    in_buf,
+    total_ref,
+    mm_ref,
+    rr_ref,
+    bb_ref,
+    spread_buf,
+    send_sem,
+    recv_sem,
+    send2_sem,
+    recv2_sem,
+    pair_send,
+    pair_recv,
+):
+    angles = w_ref.shape[0]
+    depth = vol_ref.shape[0]
+    tiles = vol_ref.shape[2] // TILE
+    slots = idx_ref.shape[0] // (angles * tiles)
+    half = meas_ref.shape[2] // 2
+    per = half // TILE
+    k = lax.axis_index("gz")
+    other = 1 - k
+    me = lax.axis_index("gy") * 2 + k
+
+    def device(d):
+        return {"gy": d // 2, "gz": lax.rem(d, 2)}
+
+    barrier = pltpu.get_barrier_semaphore()
+
+    def greet(i, carry):
+        d = lax.rem(me + i, count)
+        pl.semaphore_signal(barrier, inc=1, device_id=device(d), device_id_type=MESH)
+        return carry
+
+    lax.fori_loop(1, count, greet, 0)
+
+    column_sums(w_ref, vol_ref, lhs_ref)
+    all_products(lhs_ref, fp_ref, prod_ref, False)
+
+    pl.semaphore_wait(barrier, count - 1)
+
+    mine = pl.ds(pl.multiple_of(k * half, half), half)
+    theirs = pl.ds(pl.multiple_of(other * half, half), half)
+
+    def pair(n, src, dst):
+        return pltpu.make_async_remote_copy(
+            src_ref=src,
+            dst_ref=dst,
+            send_sem=pair_send.at[n],
+            recv_sem=pair_recv.at[n],
+            device_id={"gz": other},
+            device_id_type=MESH,
+        )
+
+    pair_m = pair(0, meas_ref.at[:, :, theirs], mm_ref.at[k])
+    pair_r = pair(1, ray_ref.at[:, :, theirs], rr_ref.at[k])
+    pair_m.start()
+    pair_r.start()
+    mm_ref[k] = meas_ref[:, :, mine]
+    rr_ref[k] = ray_ref[:, :, mine]
+
+    def scatter_copy(d, slot):
+        return pltpu.make_async_remote_copy(
+            src_ref=out_buf.at[d],
+            dst_ref=in_buf.at[slot],
+            send_sem=send_sem.at[d],
+            recv_sem=recv_sem.at[slot],
+            device_id=device(d),
+            device_id_type=MESH,
+        )
+
+    def block(d):
+        return jnp.concatenate(
+            [ray_sum(idx_ref, prod_ref, d * per + h, angles, tiles, slots) for h in range(per)],
+            axis=1,
+        )
+
+    def project(i, carry):
+        d = lax.rem(me + i, count)
+        out_buf[d] = block(d).astype(jnp.bfloat16)
+        scatter_copy(d, me).start()
+        return carry
+
+    lax.fori_loop(1, count, project, 0)
+    total_ref[other] = jnp.zeros(total_ref.shape[1:], jnp.float32)
+    total_ref[k] = block(me)
+
+    def collect(i, carry):
+        s = lax.rem(me + count - i, count)
+        scatter_copy(s, s).wait_recv()
+        row = lax.rem(s, 2)
+        total_ref[row] = total_ref[row] + in_buf[s].astype(jnp.float32)
+        return carry
+
+    lax.fori_loop(1, count, collect, 0)
+
+    pair_m.wait_recv()
+    pair_r.wait_recv()
+    lows, highs = [], []
+    for a in range(angles):
+        at = slice(a * depth, (a + 1) * depth)
+        ext = ext_ref[a : a + 1, mine]
+        gates = [jnp.where(ext >= h, c, 0.0) for h, c in enumerate(CONE_WEIGHTS, 1)]
+        projected = jnp.concatenate([total_ref[0, at], total_ref[1, at]], axis=0)
+        measured = jnp.concatenate([mm_ref[0, a], mm_ref[1, a]], axis=0)
+        ray = jnp.concatenate([rr_ref[0, a], rr_ref[1, a]], axis=0)
+        rows = cone_rows((measured - cone_rows(projected, gates)) / ray, gates)
+        bb_ref[0, a] = rows[:depth]
+        bb_ref[1, a] = rows[depth:]
+        lows.append(rows[:depth])
+        highs.append(rows[depth:])
+    spread_buf[0] = jnp.concatenate(lows, axis=0).astype(jnp.bfloat16)
+    spread_buf[1] = jnp.concatenate(highs, axis=0).astype(jnp.bfloat16)
+
+    def gather_copy(d, slot):
+        return pltpu.make_async_remote_copy(
+            src_ref=spread_buf.at[lax.rem(d, 2)],
+            dst_ref=sent_ref.at[slot],
+            send_sem=send2_sem.at[d],
+            recv_sem=recv2_sem.at[slot],
+            device_id=device(d),
+            device_id_type=MESH,
+        )
+
+    def gather_start(i, carry):
+        gather_copy(lax.rem(me + i, count), me).start()
+        return carry
+
+    lax.fori_loop(1, count, gather_start, 0)
+    pair_b = pair(2, bb_ref.at[other], back_ref.at[:, :, mine])
+    pair_b.start()
+    back_ref[:, :, mine] = bb_ref[k]
+    sent_ref[me] = spread_buf[k]
+
+    def finish(i, carry):
+        s = lax.rem(me + count - i, count)
+        gather_copy(s, s).wait_recv()
+        return carry
+
+    lax.fori_loop(1, count, finish, 0)
+
+    def drain(i, carry):
+        d = lax.rem(me + i, count)
+        scatter_copy(d, me).wait_send()
+        gather_copy(d, me).wait_send()
+        return carry
+
+    lax.fori_loop(1, count, drain, 0)
+    pair_b.wait_recv()
+    pair_m.wait_send()
+    pair_r.wait_send()
+    pair_b.wait_send()
+
+
+def exchange(count, packed, column_weight, footprint, volume, extent, measured, ray):
+    angles = column_weight.shape[0]
+    depth, _, total = volume.shape
+    tiles = total // TILE
+    banks = footprint.shape[0]
+    m = angles * depth
+    half = measured.shape[2] // 2
+    pieces = (2, angles, depth, half)
+    return pl.pallas_call(
+        functools.partial(exchange_kernel, count),
+        out_shape=(
+            jax.ShapeDtypeStruct(measured.shape, jnp.float32),
+            jax.ShapeDtypeStruct((count, m, half), jnp.bfloat16),
+        ),
+        in_specs=[SMEM, SMEM, VMEM, VMEM, VMEM, VMEM, VMEM],
+        out_specs=(VMEM, VMEM),
+        scratch_shapes=[
+            pltpu.VMEM((tiles * m, TILE), jnp.bfloat16),
+            pltpu.VMEM(((banks + 1) * tiles * angles, ROWS, TILE), jnp.float32),
+            pltpu.VMEM((count, m, half), jnp.bfloat16),
+            pltpu.VMEM((count, m, half), jnp.bfloat16),
+            pltpu.VMEM((2, m, half), jnp.float32),
+            pltpu.VMEM(pieces, jnp.float32),
+            pltpu.VMEM(pieces, jnp.float32),
+            pltpu.VMEM(pieces, jnp.float32),
+            pltpu.VMEM((2, m, half), jnp.bfloat16),
+            pltpu.SemaphoreType.DMA((count,)),
+            pltpu.SemaphoreType.DMA((count,)),
+            pltpu.SemaphoreType.DMA((count,)),
+            pltpu.SemaphoreType.DMA((count,)),
+            pltpu.SemaphoreType.DMA((3,)),
+            pltpu.SemaphoreType.DMA((3,)),
+        ],
+        compiler_params=pltpu.CompilerParams(
+            collective_id=0, has_side_effects=True, vmem_limit_bytes=VMEM_LIMIT
+        ),
+        name="project_and_exchange",
+    )(packed, column_weight, footprint, volume, extent, measured, ray)
+
+
 def shards(
     volume,
     column_weight,
@@ -275,14 +494,22 @@
     angles = column_weight.shape[0]
     depth, _, total = volume.shape
     packed = packed_slots(tile_xblock, tile_bank, tile_count, footprint.shape[0])
-    partial = forward(packed, column_weight, footprint, volume).reshape(angles, depth, total)
-    owned = lax.psum_scatter(partial, "gy", scatter_dimension=2, tiled=True)
-    predicted = cone_across(owned, cone_extent)
-    back_rows = cone_across((measured - predicted) / ray_length, cone_extent)
-    sent = lax.all_gather(back_rows.astype(jnp.bfloat16), "gy", axis=2, tiled=True)
-    new_volume = back(
-        packed, column_weight, sent.reshape(1, angles * depth, total), footprint, volume
-    )
+    half = measured.shape[2] // 2
+    if lax.axis_size("gz") == 2 and half % TILE == 0:
+        count = 2 * lax.axis_size("gy")
+        back_rows, sent = exchange(
+            count, packed, column_weight, footprint, volume, cone_extent, measured, ray_length
+        )
+        new_volume = back(packed, column_weight, sent, footprint, volume)
+    else:
+        partial = forward(packed, column_weight, footprint, volume).reshape(angles, depth, total)
+        owned = lax.psum_scatter(partial, "gy", scatter_dimension=2, tiled=True)
+        predicted = cone_across(owned, cone_extent)
+        back_rows = cone_across((measured - predicted) / ray_length, cone_extent)
+        sent = lax.all_gather(back_rows.astype(jnp.bfloat16), "gy", axis=2, tiled=True)
+        new_volume = back(
+            packed, column_weight, sent.reshape(1, angles * depth, total), footprint, volume
+        )
     return new_volume, back_rows
 
 

time: 142 us -> 35.5 us (0.25)
  the two profiles are of different devices: /device:TPU:0 before, /device:TPU:25 now
where the time goes in v2:
time: 35.5 us; the launch traced here: 35.1 us
  Pallas kernels  28.8 us (81%)
  local copies, waits for them, and re-layouts  4.73 us (13%)
  other arithmetic  0.82 us (2%)
  between operations  0.74 us (2%)
    pallas_call x1, Pallas kernels, exchange(): pl.pallas_call(functools.partial(exchange_kernel, count), out_shape=(jax....  21.4 us
    pallas_call x1, Pallas kernels, back(): pl.pallas_call(back_kernel, out_shape=jax.ShapeDtypeStruct(volume.shape,...  7.43 us
    unnamed x18, local copies, waits for them, and re-layouts  4.08 us
    mul x1, other arithmetic, packed_slots(): return (b * (tiles * angles) + xblock[:, 0] * angles + angle).reshape(-1)  0.72 us

profile of v2, /device:TPU:25, one launch (start us, length us, event | category | flops | bytes accessed | tf_op | source)
XLA Modules:
  0.0 35.1 jit_solution(2555952680234829557)
XLA Ops:
  0.6 0.0 copy-start.7
  0.6 0.7 %broadcast_multiply_fusion = s32[4,1,32,6]{2,1,3,0:T(1,128)S(1)} fusion(s32[4,1,32,6]{2,1,3,0:T(1,128)} %param.11), kind=kLoop, calls=%fused_computation.1 | loop fusion | flops 768 | bytes 6144 | tf_op jit(solution)/shard_map/mul | solution.py:139
  1.4 0.0 copy-done.7
  1.4 0.1 iota_compare_fusion
  1.5 0.1 lt.23
  1.6 0.1 copy.12
  1.7 0.0 copy-start.6
  1.7 0.1 mul.21
  1.9 0.6 %copy-done.6 = s32[4,1,32,6]{2,1,3,0:T(1,128)S(1)} copy-done((s32[4,1,32,6]{2,1,3,0:T(1,128)S(1)}, s32[4,1,32,6]{2,1,3,0:T(1,128)}, u32[]{:S(2)}) %copy-start.6) | copy-done | bytes 3096
  2.4 0.1 copy.11
  2.5 0.1 squeeze.4
  2.7 0.0 copy-start.2
  2.7 0.0 copy-start.3
  2.7 0.1 add.17
  2.9 0.0 copy-start.4
  2.9 0.0 copy-start.5
  2.9 0.6 %copy-done.2 = f32[4,8,512]{2,1,0:T(8,128)S(1)} copy-done((f32[4,8,512]{2,1,0:T(8,128)S(1)}, f32[4,8,512]{2,1,0:T(8,128)}, u32[]{:S(2)}) %copy-start.2) | copy-done | bytes 65560
  3.5 0.0 copy-done.3
  3.6 0.0 copy-done.4
  3.6 0.0 copy-done.5
  3.6 0.0 copy-start
  3.6 1.0 %copy-done = bf16[16,128,128]{2,1,0:T(8,128)(2,1)S(1)} copy-done((bf16[16,128,128]{2,1,0:T(8,128)(2,1)S(1)}, bf16[16,128,128]{2,1,0:T(8,128)(2,1)}, u32[]{:S(2)}) %copy-start) | copy-done | bytes 524312
  4.6 0.0 copy-start.1
  4.6 1.0 %copy-done.1 = bf16[8,8,4096]{2,1,0:T(8,128)(2,1)S(1)} copy-done((bf16[8,8,4096]{2,1,0:T(8,128)(2,1)S(1)}, bf16[8,8,4096]{2,1,0:T(8,128)(2,1)}, u32[]{:S(2)}) %copy-start.1) | copy-done | bytes 524312
  5.7 21.4 %project_and_exchange.1 = (f32[4,8,512]{2,1,0:T(8,128)S(1)}, bf16[16,32,256]{2,1,0:T(8,128)(2,1)S(1)}) custom-call(s32[768]{0:T(1024)S(1)} %add_add_fusion.idx_ref, f32[4,8]{1,0:T(4,128)S(1)} %copy-done.5, bf16[16,128,128]{2,1,0:T(8,128)(2,1)S(1)} %copy-done, bf16[8,8,4096]{2,1,0:T(8,128)(2,1)S(1)} %copy-done.1, s32[4,512]{1,0:T(4,128)S(1)} %copy-done.4, ...), custom_call_target="tpu_custom_call" | custom-call | tf_op jit(solution)/shard_map/project_and_exchange/pallas_call | solution.py:451
  27.1 7.4 %back_spread.1 = bf16[8,8,4096]{2,1,0:T(8,128)(2,1)} custom-call(s32[768]{0:T(1024)S(1)} %add_add_fusion.idx_ref, f32[4,8]{1,0:T(4,128)S(1)} %copy-done.5, bf16[16,32,256]{2,1,0:T(8,128)(2,1)S(1)} %get-tuple-element.4.sent_ref, bf16[16,128,128]{2,1,0:T(8,128)(2,1)S(1)} %copy-done, bf16[8,8,4096]{2,1,0:T(8,128)(2,1)S(1)} %copy-done.1), custom_call_target="tpu_custom_call" | custom-call | tf_op jit(solution)/shard_map/back_spread/pallas_call | solution.py:213
  34.5 0.6 %copy.14 = f32[4,8,512]{2,1,0:T(8,128)} copy(f32[4,8,512]{2,1,0:T(8,128)S(1)} %get-tuple-element.9) | data formatting | bytes 131072
  (2 shorter events, 0.0 us)
Async XLA Ops:
  0.6 0.7 %copy-start.7 = (s32[4,1,32]{2,1,0:T(1,128)S(1)}, s32[4,1,32]{2,1,0:T(1,128)}, u32[]{:S(2)}) copy-start(s32[4,1,32]{2,1,0:T(1,128)} %param.13) | copy-start | bytes 1540
  1.7 0.7 %copy-start.6 = (s32[4,1,32,6]{2,1,3,0:T(1,128)S(1)}, s32[4,1,32,6]{2,1,3,0:T(1,128)}, u32[]{:S(2)}) copy-start(s32[4,1,32,6]{2,1,3,0:T(1,128)} %param.12) | copy-start | bytes 9220
  2.7 0.8 %copy-start.2 = (f32[4,8,512]{2,1,0:T(8,128)S(1)}, f32[4,8,512]{2,1,0:T(8,128)}, u32[]{:S(2)}) copy-start(f32[4,8,512]{2,1,0:T(8,128)} %meas_ref.1) | copy-start | bytes 196612
  2.7 0.9 %copy-start.3 = (f32[4,8,512]{2,1,0:T(8,128)S(1)}, f32[4,8,512]{2,1,0:T(8,128)}, u32[]{:S(2)}) copy-start(f32[4,8,512]{2,1,0:T(8,128)} %ray_ref.1) | copy-start | bytes 196612
  2.9 0.7 %copy-start.4 = (s32[4,512]{1,0:T(4,128)S(1)}, s32[4,512]{1,0:T(4,128)}, u32[]{:S(2)}) copy-start(s32[4,512]{1,0:T(4,128)} %ext_ref.1) | copy-start | bytes 24580
  2.9 0.7 %copy-start.5 = (f32[4,8]{1,0:T(4,128)S(1)}, f32[4,8]{1,0:T(4,128)}, u32[]{:S(2)}) copy-start(f32[4,8]{1,0:T(4,128)} %w_ref.3) | copy-start | bytes 388
  3.6 1.0 %copy-start = (bf16[16,128,128]{2,1,0:T(8,128)(2,1)S(1)}, bf16[16,128,128]{2,1,0:T(8,128)(2,1)}, u32[]{:S(2)}) copy-start(bf16[16,128,128]{2,1,0:T(8,128)(2,1)} %fp_ref.3) | copy-start | bytes 1572868
  4.6 1.0 %copy-start.1 = (bf16[8,8,4096]{2,1,0:T(8,128)(2,1)S(1)}, bf16[8,8,4096]{2,1,0:T(8,128)(2,1)}, u32[]{:S(2)}) copy-start(bf16[8,8,4096]{2,1,0:T(8,128)(2,1)} %vol_ref.3) | copy-start | bytes 1572868

commit v3 on v2

--- a/solution.py
+++ b/solution.py
@@ -123,8 +123,7 @@
 def ray_sum(idx_ref, prod_ref, t, angles, tiles, slots):
     parts = []
     for a in range(angles):
-        at = (a * tiles + t) * slots
-        terms = [prod_ref[idx_ref[at + s]] for s in range(slots)]
+        terms = [prod_ref[idx_ref[a * tiles + t, s]] for s in range(slots)]
         while len(terms) > 1:
             terms = [sum(terms[i : i + 2][1:], terms[i]) for i in range(0, len(terms), 2)]
         parts.append(terms[0])
@@ -136,14 +135,30 @@
     used = jnp.arange(slots)[None, None, :] < count[:, 0, :, None]
     b = jnp.where(used, bank[:, 0], banks)
     angle = jnp.arange(angles, dtype=jnp.int32)[:, None, None]
-    return (b * (tiles * angles) + xblock[:, 0] * angles + angle).reshape(-1)
-
-
-def back_kernel(idx_ref, w_ref, sent_ref, fp_ref, vol_ref, out_ref, lhs_ref, prod_ref, *acc_refs):
+    return (b * (tiles * angles) + xblock[:, 0] * angles + angle).reshape(-1, slots)
+
+
+def back_kernel(
+    slots,
+    table_ref,
+    w_ref,
+    sent_ref,
+    fp_ref,
+    vol_ref,
+    result_ref,
+    lhs_ref,
+    prod_ref,
+    idx_ref,
+    out_ref,
+    idx_sem,
+    out_sem,
+    *acc_refs,
+):
+    table = pltpu.make_async_copy(table_ref, idx_ref, idx_sem)
+    table.start()
     angles, cols = w_ref.shape
     depth, _, total = vol_ref.shape
     tiles = total // TILE
-    slots = idx_ref.shape[0] // (angles * tiles)
     m = angles * depth
     per = sent_ref.shape[2] // TILE
     for t in range(tiles):
@@ -152,11 +167,12 @@
     for acc in acc_refs:
         acc[...] = jnp.zeros_like(acc)
     mask = tiles * angles - 1
+    table.wait()
 
     def body(t, carry):
         for s in range(slots):
             for a in range(angles):
-                packed = idx_ref[(a * tiles + t) * slots + s]
+                packed = idx_ref[a * tiles + t, s]
                 low = packed & mask
                 x = low >> (angles.bit_length() - 1)
                 acc_refs[a][x] += prod_ref[packed - low + (t * angles + a)]
@@ -178,6 +194,10 @@
     w3 = split_part(w, jnp.where(col >= 2 * m, 1, 0))
     step = 4
 
+    def piece(i):
+        at = pl.ds(pl.multiple_of(i * step * TILE, step * TILE), step * TILE)
+        return pltpu.make_async_copy(out_ref.at[:, :, at], result_ref.at[:, :, at], out_sem.at[i])
+
     def finish(i, carry):
         s = jnp.concatenate(
             [
@@ -195,29 +215,37 @@
         for z in range(depth):
             fresh = vol_ref[z, :, at].astype(jnp.float32) + change[z * cols : (z + 1) * cols]
             out_ref[z, :, at] = jnp.maximum(fresh, 0.0).astype(jnp.bfloat16)
+        piece(i).start()
         return carry
 
     lax.fori_loop(0, tiles // step, finish, 0)
+    for i in range(tiles // step):
+        piece(i).wait()
 
 
 SMEM = pl.BlockSpec(memory_space=pltpu.SMEM)
 VMEM = pl.BlockSpec(memory_space=pltpu.VMEM)
-
-
-def back(packed, column_weight, sent, footprint, volume):
+HBM = pl.BlockSpec(memory_space=pltpu.HBM)
+
+
+def back(slots, packed, column_weight, sent, footprint, volume):
     angles = column_weight.shape[0]
     depth, _, total = volume.shape
     tiles = total // TILE
     banks = footprint.shape[0]
     rows = tiles * angles * depth
     return pl.pallas_call(
-        back_kernel,
+        functools.partial(back_kernel, slots),
         out_shape=jax.ShapeDtypeStruct(volume.shape, jnp.bfloat16),
-        in_specs=[SMEM, SMEM, VMEM, VMEM, VMEM],
-        out_specs=VMEM,
+        in_specs=[HBM, SMEM, VMEM, VMEM, VMEM],
+        out_specs=HBM,
         scratch_shapes=[
             pltpu.VMEM((rows, TILE), jnp.bfloat16),
             pltpu.VMEM(((banks + 1) * tiles * angles, ROWS, TILE), jnp.float32),
+            pltpu.SMEM(packed.shape, jnp.int32),
+            pltpu.VMEM(volume.shape, jnp.bfloat16),
+            pltpu.SemaphoreType.DMA,
+            pltpu.SemaphoreType.DMA((tiles // 4,)),
         ]
         + [pltpu.VMEM((tiles, ROWS, TILE), jnp.float32) for _ in range(angles)],
         compiler_params=pltpu.CompilerParams(vmem_limit_bytes=VMEM_LIMIT),
@@ -228,7 +256,7 @@
 def forward_kernel(idx_ref, w_ref, fp_ref, vol_ref, out_ref, lhs_ref, prod_ref):
     angles = w_ref.shape[0]
     tiles = vol_ref.shape[2] // TILE
-    slots = idx_ref.shape[0] // (angles * tiles)
+    slots = idx_ref.shape[1]
     column_sums(w_ref, vol_ref, lhs_ref)
     all_products(lhs_ref, fp_ref, prod_ref, False)
 
@@ -275,15 +303,29 @@
 
 def exchange_kernel(
     count,
-    idx_ref,
     w_ref,
+    xblock_hbm,
+    bank_hbm,
+    filled_hbm,
+    fp_hbm,
+    vol_hbm,
+    ext_hbm,
+    meas_hbm,
+    ray_hbm,
+    back_ref,
+    sent_ref,
+    table_hbm,
+    xblock_ref,
+    bank_ref,
+    filled_ref,
     fp_ref,
     vol_ref,
     ext_ref,
     meas_ref,
     ray_ref,
-    back_ref,
-    sent_ref,
+    table_ref,
+    idx_ref,
+    load_sem,
     lhs_ref,
     prod_ref,
     out_buf,
@@ -303,7 +345,8 @@
     angles = w_ref.shape[0]
     depth = vol_ref.shape[0]
     tiles = vol_ref.shape[2] // TILE
-    slots = idx_ref.shape[0] // (angles * tiles)
+    slots = xblock_ref.shape[3]
+    banks = fp_ref.shape[0]
     half = meas_ref.shape[2] // 2
     per = half // TILE
     k = lax.axis_index("gz")
@@ -313,6 +356,23 @@
     def device(d):
         return {"gy": d // 2, "gz": lax.rem(d, 2)}
 
+    loads = [
+        pltpu.make_async_copy(src, dst, load_sem.at[n])
+        for n, (src, dst) in enumerate(
+            (
+                (vol_hbm, vol_ref),
+                (fp_hbm, fp_ref),
+                (xblock_hbm, xblock_ref),
+                (bank_hbm, bank_ref),
+                (filled_hbm, filled_ref),
+                (ext_hbm, ext_ref),
+                (meas_hbm, meas_ref),
+                (ray_hbm, ray_ref),
+            )
+        )
+    ]
+    for load in loads:
+        load.start()
     barrier = pltpu.get_barrier_semaphore()
 
     def greet(i, carry):
@@ -322,8 +382,32 @@
 
     lax.fori_loop(1, count, greet, 0)
 
+    for load in loads[2:5]:
+        load.wait()
+    table_ref[...] = jnp.zeros_like(table_ref)
+    lane = lax.broadcasted_iota(jnp.int32, (tiles, slots), 1)
+    square = (tiles, tiles)
+    eye = lax.broadcasted_iota(jnp.int32, square, 0) == lax.broadcasted_iota(jnp.int32, square, 1)
+    for a in range(angles):
+        filled = jnp.broadcast_to(filled_ref[a].astype(jnp.float32), square)
+        filled = jnp.sum(jnp.where(eye, filled, 0.0), axis=1, keepdims=True)
+        bank = jnp.where(lane.astype(jnp.float32) < filled, bank_ref[a, 0], banks)
+        table_ref[a * tiles : (a + 1) * tiles, :slots] = (
+            bank * (tiles * angles) + xblock_ref[a, 0] * angles + a
+        )
+    tables = (
+        pltpu.make_async_copy(table_ref, idx_ref, load_sem.at[len(loads)]),
+        pltpu.make_async_copy(table_ref, table_hbm, load_sem.at[len(loads) + 1]),
+    )
+    for table in tables:
+        table.start()
+
+    loads[0].wait()
     column_sums(w_ref, vol_ref, lhs_ref)
+    loads[1].wait()
     all_products(lhs_ref, fp_ref, prod_ref, False)
+    for waited in loads[5:] + list(tables):
+        waited.wait()
 
     pl.semaphore_wait(barrier, count - 1)
 
@@ -440,7 +524,10 @@
     pair_b.wait_send()
 
 
-def exchange(count, packed, column_weight, footprint, volume, extent, measured, ray):
+def exchange(
+    count, column_weight, xblock, bank, filled, footprint, volume, extent, measured, ray
+):
+    operands = (xblock, bank, filled, footprint, volume, extent, measured, ray)
     angles = column_weight.shape[0]
     depth, _, total = volume.shape
     tiles = total // TILE
@@ -453,10 +540,15 @@
         out_shape=(
             jax.ShapeDtypeStruct(measured.shape, jnp.float32),
             jax.ShapeDtypeStruct((count, m, half), jnp.bfloat16),
+            jax.ShapeDtypeStruct((angles * tiles, TILE), jnp.int32),
         ),
-        in_specs=[SMEM, SMEM, VMEM, VMEM, VMEM, VMEM, VMEM],
-        out_specs=(VMEM, VMEM),
-        scratch_shapes=[
+        in_specs=[SMEM] + [HBM] * len(operands),
+        out_specs=(VMEM, VMEM, HBM),
+        scratch_shapes=[pltpu.VMEM(x.shape, x.dtype) for x in operands]
+        + [
+            pltpu.VMEM((angles * tiles, TILE), jnp.int32),
+            pltpu.SMEM((angles * tiles, TILE), jnp.int32),
+            pltpu.SemaphoreType.DMA((len(operands) + 2,)),
             pltpu.VMEM((tiles * m, TILE), jnp.bfloat16),
             pltpu.VMEM(((banks + 1) * tiles * angles, ROWS, TILE), jnp.float32),
             pltpu.VMEM((count, m, half), jnp.bfloat16),
@@ -477,7 +569,7 @@
             collective_id=0, has_side_effects=True, vmem_limit_bytes=VMEM_LIMIT
         ),
         name="project_and_exchange",
-    )(packed, column_weight, footprint, volume, extent, measured, ray)
+    )(column_weight, *operands)
 
 
 def shards(
@@ -493,22 +585,33 @@
 ):
     angles = column_weight.shape[0]
     depth, _, total = volume.shape
-    packed = packed_slots(tile_xblock, tile_bank, tile_count, footprint.shape[0])
+    slots = tile_xblock.shape[3]
     half = measured.shape[2] // 2
     if lax.axis_size("gz") == 2 and half % TILE == 0:
         count = 2 * lax.axis_size("gy")
-        back_rows, sent = exchange(
-            count, packed, column_weight, footprint, volume, cone_extent, measured, ray_length
-        )
-        new_volume = back(packed, column_weight, sent, footprint, volume)
+        back_rows, sent, packed = exchange(
+            count,
+            column_weight,
+            tile_xblock,
+            tile_bank,
+            tile_count,
+            footprint,
+            volume,
+            cone_extent,
+            measured,
+            ray_length,
+        )
+        new_volume = back(slots, packed, column_weight, sent, footprint, volume)
     else:
+        packed = packed_slots(tile_xblock, tile_bank, tile_count, footprint.shape[0])
         partial = forward(packed, column_weight, footprint, volume).reshape(angles, depth, total)
         owned = lax.psum_scatter(partial, "gy", scatter_dimension=2, tiled=True)
         predicted = cone_across(owned, cone_extent)
         back_rows = cone_across((measured - predicted) / ray_length, cone_extent)
         sent = lax.all_gather(back_rows.astype(jnp.bfloat16), "gy", axis=2, tiled=True)
+        packed = jnp.pad(packed, ((0, 0), (0, TILE - slots)))
         new_volume = back(
-            packed, column_weight, sent.reshape(1, angles * depth, total), footprint, volume
+            slots, packed, column_weight, sent.reshape(1, angles * depth, total), footprint, volume
         )
     return new_volume, back_rows
 

time: 35.5 us -> 34.8 us (0.980)
  other arithmetic: 0.82 us -> 0 us
  Pallas kernels: 28.8 us -> 29.3 us
    mul x1 -> x0, other arithmetic: 0.72 us -> none  [packed_slots(): return (b * (tiles * angles) + xblock[:, 0] * angles + angle).reshape(-1)]
    pallas_call x1, Pallas kernels: 21.4 us -> 22 us  [exchange(): pl.pallas_call(functools.partial(exchange_kernel, count), out_shape=(jax....]
    unnamed x18 -> x21, local copies, waits for them, and re-layouts: 4.08 us -> 4.41 us
where the time goes in v3:
time: 34.8 us; the launch traced here: 34.5 us
  Pallas kernels  29.3 us (84%)
  local copies, waits for them, and re-layouts  4.41 us (13%)
  between operations  0.74 us (2%)
    pallas_call x1, Pallas kernels, exchange(): pl.pallas_call(functools.partial(exchange_kernel, count), out_shape=(jax....  22 us
    pallas_call x1, Pallas kernels, back(): pl.pallas_call(functools.partial(back_kernel, slots), out_shape=jax.Shape...  7.31 us
    unnamed x21, local copies, waits for them, and re-layouts  4.41 us

profile of v3, /device:TPU:25, one launch (start us, length us, event | category | flops | bytes accessed | tf_op | source)
XLA Modules:
  0.0 34.5 jit_solution(5070676689371549411)
XLA Ops:
  0.6 0.0 copy-start.5
  0.6 0.0 copy-start.4
  0.7 0.8 %copy.11.xblock_hbm = s32[4,1,32,6]{3,2,1,0:T(8,128)S(1)} copy(s32[4,1,32,6]{2,1,3,0:T(1,128)} %param.11) | data formatting | bytes 6144 | tf_op args[2]
  1.5 0.0 copy-start.6
  1.5 0.0 copy-start.7
  1.5 0.0 copy-start.8
  1.5 0.8 %copy.12.bank_hbm = s32[4,1,32,6]{3,2,1,0:T(8,128)S(1)} copy(s32[4,1,32,6]{2,1,3,0:T(1,128)} %param.12) | data formatting | bytes 6144 | tf_op args[3]
  2.3 0.0 copy-done.5
  2.3 0.0 copy-done.4
  2.4 0.0 copy-done.6
  2.4 0.0 copy-done.7
  2.4 0.0 copy-done.8
  2.4 0.0 copy-start
  2.4 1.0 %copy-done = bf16[16,128,128]{2,1,0:T(8,128)(2,1)S(1)} copy-done((bf16[16,128,128]{2,1,0:T(8,128)(2,1)S(1)}, bf16[16,128,128]{2,1,0:T(8,128)(2,1)}, u32[]{:S(2)}) %copy-start) | copy-done | bytes 524312
  3.4 0.0 copy-start.2
  3.4 1.0 %copy-done.2 = bf16[8,8,4096]{2,1,0:T(8,128)(2,1)S(1)} copy-done((bf16[8,8,4096]{2,1,0:T(8,128)(2,1)S(1)}, bf16[8,8,4096]{2,1,0:T(8,128)(2,1)}, u32[]{:S(2)}) %copy-start.2) | copy-done | bytes 524312
  4.5 0.0 copy-start.1
  4.5 0.0 copy-start.3
  4.5 22.0 %project_and_exchange.1 = (f32[4,8,512]{2,1,0:T(8,128)S(1)}, bf16[16,32,256]{2,1,0:T(8,128)(2,1)S(1)}, s32[128,128]{1,0:T(8,128)S(1)}) custom-call(f32[4,8]{1,0:T(4,128)S(1)} %copy-done.7, s32[4,1,32,6]{3,2,1,0:T(8,128)S(1)} %copy.11.xblock_hbm, s32[4,1,32,6]{3,2,1,0:T(8,128)S(1)} %copy.12.bank_hbm, s32[4,1,32]{2,1,0:T(1,128)S(1)} %copy-done.8, ...), custom_call_target="tpu_custom_call" | custom-call | tf_op jit(solution)/shard_map/project_and_exchange/pallas_call | solution.py:538
  26.5 0.0 copy-done.1
  26.5 0.0 copy-done.3
  26.5 7.3 %back_spread.1 = bf16[8,8,4096]{2,1,0:T(8,128)(2,1)} custom-call(s32[128,128]{1,0:T(8,128)S(1)} %get-tuple-element.5.table_ref, f32[4,8]{1,0:T(4,128)S(1)} %copy-done.7, bf16[16,32,256]{2,1,0:T(8,128)(2,1)S(1)} %get-tuple-element.6.sent_ref, bf16[16,128,128]{2,1,0:T(8,128)(2,1)S(1)} %copy-done.1, bf16[8,8,4096]{2,1,0:T(8,128)(2,1)S(1)} %copy-done.3), custom_call_target="tpu_custom_call" | custom-call | tf_op jit(solution)/shard_map/back_spread/pallas_call | solution.py:237
  33.8 0.6 %copy.14 = f32[4,8,512]{2,1,0:T(8,128)} copy(f32[4,8,512]{2,1,0:T(8,128)S(1)} %get-tuple-element.11) | data formatting | bytes 131072
Async XLA Ops:
  0.6 1.7 %copy-start.5 = (f32[4,8,512]{2,1,0:T(8,128)S(1)}, f32[4,8,512]{2,1,0:T(8,128)}, u32[]{:S(2)}) copy-start(f32[4,8,512]{2,1,0:T(8,128)} %ray_hbm.1) | copy-start | bytes 196612
  0.6 1.7 %copy-start.4 = (f32[4,8,512]{2,1,0:T(8,128)S(1)}, f32[4,8,512]{2,1,0:T(8,128)}, u32[]{:S(2)}) copy-start(f32[4,8,512]{2,1,0:T(8,128)} %meas_hbm.1) | copy-start | bytes 196612
  1.5 0.9 %copy-start.6 = (s32[4,512]{1,0:T(4,128)S(1)}, s32[4,512]{1,0:T(4,128)}, u32[]{:S(2)}) copy-start(s32[4,512]{1,0:T(4,128)} %ext_hbm.1) | copy-start | bytes 24580
  1.5 0.9 %copy-start.7 = (f32[4,8]{1,0:T(4,128)S(1)}, f32[4,8]{1,0:T(4,128)}, u32[]{:S(2)}) copy-start(f32[4,8]{1,0:T(4,128)} %w_ref.3) | copy-start | bytes 388
  1.5 0.9 %copy-start.8 = (s32[4,1,32]{2,1,0:T(1,128)S(1)}, s32[4,1,32]{2,1,0:T(1,128)}, u32[]{:S(2)}) copy-start(s32[4,1,32]{2,1,0:T(1,128)} %filled_hbm.1) | copy-start | bytes 1540
  2.4 1.0 %copy-start = (bf16[16,128,128]{2,1,0:T(8,128)(2,1)S(1)}, bf16[16,128,128]{2,1,0:T(8,128)(2,1)}, u32[]{:S(2)}) copy-start(bf16[16,128,128]{2,1,0:T(8,128)(2,1)} %fp_ref.1) | copy-start | bytes 1572868
  3.4 1.0 %copy-start.2 = (bf16[8,8,4096]{2,1,0:T(8,128)(2,1)S(1)}, bf16[8,8,4096]{2,1,0:T(8,128)(2,1)}, u32[]{:S(2)}) copy-start(bf16[8,8,4096]{2,1,0:T(8,128)(2,1)} %vol_ref.1) | copy-start | bytes 1572868
  4.5 22.0 %copy-start.1 = (bf16[16,128,128]{2,1,0:T(8,128)(2,1)S(1)}, bf16[16,128,128]{2,1,0:T(8,128)(2,1)}, u32[]{:S(2)}) copy-start(bf16[16,128,128]{2,1,0:T(8,128)(2,1)} %fp_ref.1) | copy-start | bytes 1572868
  4.5 22.0 %copy-start.3 = (bf16[8,8,4096]{2,1,0:T(8,128)(2,1)S(1)}, bf16[8,8,4096]{2,1,0:T(8,128)(2,1)}, u32[]{:S(2)}) copy-start(bf16[8,8,4096]{2,1,0:T(8,128)(2,1)} %vol_ref.1) | copy-start | bytes 1572868

commit v4 on v3

--- a/solution.py
+++ b/solution.py
@@ -1,4 +1,5 @@
 import functools
+import math
 
 import jax
 import jax.numpy as jnp
@@ -10,7 +11,7 @@
 TILE = 128
 ROWS = 8
 CONE_WEIGHTS = (0.45, 0.3, 0.2, 0.12)
-VMEM_LIMIT = 48 * 2**20
+VMEM_LIMIT = 64 * 2**20 - 2**18
 MESH = pl.DeviceIdType.MESH
 
 
@@ -123,7 +124,7 @@
 def ray_sum(idx_ref, prod_ref, t, angles, tiles, slots):
     parts = []
     for a in range(angles):
-        terms = [prod_ref[idx_ref[a * tiles + t, s]] for s in range(slots)]
+        terms = [prod_ref[idx_ref[a * slots + s, t]] for s in range(slots)]
         while len(terms) > 1:
             terms = [sum(terms[i : i + 2][1:], terms[i]) for i in range(0, len(terms), 2)]
         parts.append(terms[0])
@@ -131,38 +132,62 @@
 
 
 def packed_slots(xblock, bank, count, banks):
-    angles, _, tiles, slots = xblock.shape
-    used = jnp.arange(slots)[None, None, :] < count[:, 0, :, None]
-    b = jnp.where(used, bank[:, 0], banks)
-    angle = jnp.arange(angles, dtype=jnp.int32)[:, None, None]
-    return (b * (tiles * angles) + xblock[:, 0] * angles + angle).reshape(-1, slots)
+    angles, slots, _, tiles = xblock.shape
+    used = jnp.arange(slots)[None, :, None, None] < count[:, None]
+    b = jnp.where(used, bank, banks)
+    angle = jnp.arange(angles, dtype=jnp.int32)[:, None, None, None]
+    packed = (b * (tiles * angles) + xblock * angles + angle).reshape(angles * slots, tiles)
+    return jnp.pad(packed, ((0, 0), (0, TILE - tiles)))
 
 
 def back_kernel(
-    slots,
     table_ref,
     w_ref,
-    sent_ref,
+    sent_hbm,
+    fp_hbm,
+    vol_hbm,
+    rows_in_ref,
+    result_ref,
+    rows_out_ref,
+    lhs_ref,
+    prod_ref,
     fp_ref,
     vol_ref,
-    result_ref,
-    lhs_ref,
-    prod_ref,
+    sent_ref,
     idx_ref,
     out_ref,
-    idx_sem,
+    load_sem,
+    sent_sem,
     out_sem,
     *acc_refs,
 ):
-    table = pltpu.make_async_copy(table_ref, idx_ref, idx_sem)
-    table.start()
+    sources = sent_hbm.shape[0]
+    batches = math.gcd(sources, 4)
+    group = sources // batches
+    arrivals = []
+    for n in range(batches):
+        at = pl.ds(n * group, group)
+        arrivals.append(
+            pltpu.make_async_copy(sent_hbm.at[at], sent_ref.at[at], sent_sem.at[n])
+        )
+        arrivals[n].start()
+    footprints = pltpu.make_async_copy(fp_hbm, fp_ref, load_sem.at[0])
+    table = pltpu.make_async_copy(table_ref, idx_ref, load_sem.at[1])
+    columns = pltpu.make_async_copy(vol_hbm, vol_ref, load_sem.at[2])
+    rows_out = pltpu.make_async_copy(rows_in_ref, rows_out_ref, load_sem.at[3])
+    for load in (footprints, table, columns, rows_out):
+        load.start()
     angles, cols = w_ref.shape
     depth, _, total = vol_ref.shape
     tiles = total // TILE
+    slots = idx_ref.shape[0] // angles
     m = angles * depth
     per = sent_ref.shape[2] // TILE
     for t in range(tiles):
+        if t % (per * group) == 0:
+            arrivals[t // (per * group)].wait()
         lhs_ref[t * m : (t + 1) * m, :] = sent_ref[t // per, :, (t % per) * TILE : (t % per + 1) * TILE]
+    footprints.wait()
     all_products(lhs_ref, fp_ref, prod_ref, True)
     for acc in acc_refs:
         acc[...] = jnp.zeros_like(acc)
@@ -172,7 +197,7 @@
     def body(t, carry):
         for s in range(slots):
             for a in range(angles):
-                packed = idx_ref[a * tiles + t, s]
+                packed = idx_ref[a * slots + s, t]
                 low = packed & mask
                 x = low >> (angles.bit_length() - 1)
                 acc_refs[a][x] += prod_ref[packed - low + (t * angles + a)]
@@ -194,6 +219,8 @@
     w3 = split_part(w, jnp.where(col >= 2 * m, 1, 0))
     step = 4
 
+    columns.wait()
+
     def piece(i):
         at = pl.ds(pl.multiple_of(i * step * TILE, step * TILE), step * TILE)
         return pltpu.make_async_copy(out_ref.at[:, :, at], result_ref.at[:, :, at], out_sem.at[i])
@@ -221,6 +248,7 @@
     lax.fori_loop(0, tiles // step, finish, 0)
     for i in range(tiles // step):
         piece(i).wait()
+    rows_out.wait()
 
 
 SMEM = pl.BlockSpec(memory_space=pltpu.SMEM)
@@ -228,35 +256,42 @@
 HBM = pl.BlockSpec(memory_space=pltpu.HBM)
 
 
-def back(slots, packed, column_weight, sent, footprint, volume):
+def back(packed, column_weight, sent, footprint, volume, back_rows):
     angles = column_weight.shape[0]
     depth, _, total = volume.shape
     tiles = total // TILE
     banks = footprint.shape[0]
     rows = tiles * angles * depth
     return pl.pallas_call(
-        functools.partial(back_kernel, slots),
-        out_shape=jax.ShapeDtypeStruct(volume.shape, jnp.bfloat16),
-        in_specs=[HBM, SMEM, VMEM, VMEM, VMEM],
-        out_specs=HBM,
+        back_kernel,
+        out_shape=(
+            jax.ShapeDtypeStruct(volume.shape, jnp.bfloat16),
+            jax.ShapeDtypeStruct(back_rows.shape, jnp.float32),
+        ),
+        in_specs=[HBM, SMEM, HBM, HBM, HBM, HBM],
+        out_specs=(HBM, HBM),
         scratch_shapes=[
             pltpu.VMEM((rows, TILE), jnp.bfloat16),
             pltpu.VMEM(((banks + 1) * tiles * angles, ROWS, TILE), jnp.float32),
+            pltpu.VMEM(footprint.shape, jnp.bfloat16),
+            pltpu.VMEM(volume.shape, jnp.bfloat16),
+            pltpu.VMEM(sent.shape, jnp.bfloat16),
             pltpu.SMEM(packed.shape, jnp.int32),
             pltpu.VMEM(volume.shape, jnp.bfloat16),
-            pltpu.SemaphoreType.DMA,
+            pltpu.SemaphoreType.DMA((4,)),
+            pltpu.SemaphoreType.DMA((4,)),
             pltpu.SemaphoreType.DMA((tiles // 4,)),
         ]
         + [pltpu.VMEM((tiles, ROWS, TILE), jnp.float32) for _ in range(angles)],
         compiler_params=pltpu.CompilerParams(vmem_limit_bytes=VMEM_LIMIT),
         name="back_spread",
-    )(packed, column_weight, sent, footprint, volume)
+    )(packed, column_weight, sent, footprint, volume, back_rows)
 
 
 def forward_kernel(idx_ref, w_ref, fp_ref, vol_ref, out_ref, lhs_ref, prod_ref):
     angles = w_ref.shape[0]
     tiles = vol_ref.shape[2] // TILE
-    slots = idx_ref.shape[1]
+    slots = idx_ref.shape[0] // angles
     column_sums(w_ref, vol_ref, lhs_ref)
     all_products(lhs_ref, fp_ref, prod_ref, False)
 
@@ -345,7 +380,7 @@
     angles = w_ref.shape[0]
     depth = vol_ref.shape[0]
     tiles = vol_ref.shape[2] // TILE
-    slots = xblock_ref.shape[3]
+    slots = xblock_ref.shape[1]
     banks = fp_ref.shape[0]
     half = meas_ref.shape[2] // 2
     per = half // TILE
@@ -385,16 +420,12 @@
     for load in loads[2:5]:
         load.wait()
     table_ref[...] = jnp.zeros_like(table_ref)
-    lane = lax.broadcasted_iota(jnp.int32, (tiles, slots), 1)
-    square = (tiles, tiles)
-    eye = lax.broadcasted_iota(jnp.int32, square, 0) == lax.broadcasted_iota(jnp.int32, square, 1)
     for a in range(angles):
-        filled = jnp.broadcast_to(filled_ref[a].astype(jnp.float32), square)
-        filled = jnp.sum(jnp.where(eye, filled, 0.0), axis=1, keepdims=True)
-        bank = jnp.where(lane.astype(jnp.float32) < filled, bank_ref[a, 0], banks)
-        table_ref[a * tiles : (a + 1) * tiles, :slots] = (
-            bank * (tiles * angles) + xblock_ref[a, 0] * angles + a
-        )
+        for n in range(slots):
+            bank = jnp.where(n < filled_ref[a], bank_ref[a, n], banks)
+            table_ref[a * slots + n : a * slots + n + 1, :tiles] = (
+                bank * (tiles * angles) + xblock_ref[a, n] * angles + a
+            )
     tables = (
         pltpu.make_async_copy(table_ref, idx_ref, load_sem.at[len(loads)]),
         pltpu.make_async_copy(table_ref, table_hbm, load_sem.at[len(loads) + 1]),
@@ -501,8 +532,12 @@
     lax.fori_loop(1, count, gather_start, 0)
     pair_b = pair(2, bb_ref.at[other], back_ref.at[:, :, mine])
     pair_b.start()
-    back_ref[:, :, mine] = bb_ref[k]
-    sent_ref[me] = spread_buf[k]
+    kept = (
+        pltpu.make_async_copy(bb_ref.at[k], back_ref.at[:, :, mine], load_sem.at[0]),
+        pltpu.make_async_copy(spread_buf.at[k], sent_ref.at[me], load_sem.at[1]),
+    )
+    for own in kept:
+        own.start()
 
     def finish(i, carry):
         s = lax.rem(me + count - i, count)
@@ -518,6 +553,8 @@
         return carry
 
     lax.fori_loop(1, count, drain, 0)
+    for own in kept:
+        own.wait()
     pair_b.wait_recv()
     pair_m.wait_send()
     pair_r.wait_send()
@@ -527,6 +564,7 @@
 def exchange(
     count, column_weight, xblock, bank, filled, footprint, volume, extent, measured, ray
 ):
+    slots = xblock.shape[1]
     operands = (xblock, bank, filled, footprint, volume, extent, measured, ray)
     angles = column_weight.shape[0]
     depth, _, total = volume.shape
@@ -540,14 +578,14 @@
         out_shape=(
             jax.ShapeDtypeStruct(measured.shape, jnp.float32),
             jax.ShapeDtypeStruct((count, m, half), jnp.bfloat16),
-            jax.ShapeDtypeStruct((angles * tiles, TILE), jnp.int32),
+            jax.ShapeDtypeStruct((angles * slots, TILE), jnp.int32),
         ),
         in_specs=[SMEM] + [HBM] * len(operands),
-        out_specs=(VMEM, VMEM, HBM),
+        out_specs=(HBM, HBM, HBM),
         scratch_shapes=[pltpu.VMEM(x.shape, x.dtype) for x in operands]
         + [
-            pltpu.VMEM((angles * tiles, TILE), jnp.int32),
-            pltpu.SMEM((angles * tiles, TILE), jnp.int32),
+            pltpu.VMEM((angles * slots, TILE), jnp.int32),
+            pltpu.SMEM((angles * slots, TILE), jnp.int32),
             pltpu.SemaphoreType.DMA((len(operands) + 2,)),
             pltpu.VMEM((tiles * m, TILE), jnp.bfloat16),
             pltpu.VMEM(((banks + 1) * tiles * angles, ROWS, TILE), jnp.float32),
@@ -585,7 +623,8 @@
 ):
     angles = column_weight.shape[0]
     depth, _, total = volume.shape
-    slots = tile_xblock.shape[3]
+    tile_xblock = tile_xblock.transpose(0, 3, 1, 2)
+    tile_bank = tile_bank.transpose(0, 3, 1, 2)
     half = measured.shape[2] // 2
     if lax.axis_size("gz") == 2 and half % TILE == 0:
         count = 2 * lax.axis_size("gy")
@@ -601,7 +640,9 @@
             measured,
             ray_length,
         )
-        new_volume = back(slots, packed, column_weight, sent, footprint, volume)
+        new_volume, back_rows = back(
+            packed, column_weight, sent, footprint, volume, back_rows
+        )
     else:
         packed = packed_slots(tile_xblock, tile_bank, tile_count, footprint.shape[0])
         partial = forward(packed, column_weight, footprint, volume).reshape(angles, depth, total)
@@ -609,9 +650,9 @@
         predicted = cone_across(owned, cone_extent)
         back_rows = cone_across((measured - predicted) / ray_length, cone_extent)
         sent = lax.all_gather(back_rows.astype(jnp.bfloat16), "gy", axis=2, tiled=True)
-        packed = jnp.pad(packed, ((0, 0), (0, TILE - slots)))
-        new_volume = back(
-            slots, packed, column_weight, sent.reshape(1, angles * depth, total), footprint, volume
+        sent = sent.reshape(1, angles * depth, total)
+        new_volume, back_rows = back(
+            packed, column_weight, sent, footprint, volume, back_rows
         )
     return new_volume, back_rows
 

time: 34.8 us -> 32.3 us (0.928)
  local copies, waits for them, and re-layouts: 4.41 us -> 0 us
  Pallas kernels: 29.3 us -> 31.5 us
    unnamed x21 -> x0, local copies, waits for them, and re-layouts: 4.41 us -> none
    pallas_call x1, Pallas kernels: 7.31 us -> 8.83 us  [back(): pl.pallas_call(back_kernel, out_shape=(jax.ShapeDtypeStruct(volume.shape,...]
    pallas_call x1, Pallas kernels: 22 us -> 22.7 us  [exchange(): pl.pallas_call(functools.partial(exchange_kernel, count), out_shape=(jax....]
where the time goes in v4:
time: 32.3 us; the launch traced here: 32.1 us
  Pallas kernels  31.5 us (98%)
  between operations  0.64 us (2%)
    pallas_call x1, Pallas kernels, exchange(): pl.pallas_call(functools.partial(exchange_kernel, count), out_shape=(jax....  22.7 us
    pallas_call x1, Pallas kernels, back(): pl.pallas_call(back_kernel, out_shape=(jax.ShapeDtypeStruct(volume.shape,...  8.83 us

profile of v4, /device:TPU:25, one launch (start us, length us, event | category | flops | bytes accessed | tf_op | source)
XLA Modules:
  0.0 32.1 jit_solution(1668113445569762890)
XLA Ops:
  0.6 22.7 %project_and_exchange.1 = (f32[4,8,512]{2,1,0:T(8,128)}, bf16[16,32,256]{2,1,0:T(8,128)(2,1)}, s32[24,128]{1,0:T(8,128)}) custom-call(f32[4,8]{1,0:T(4,128)} %w_ref.3, s32[4,6,1,32]{3,2,1,0:T(1,128)} %bitcast.2, s32[4,6,1,32]{3,2,1,0:T(1,128)} %bitcast.3, s32[4,1,32]{2,1,0:T(1,128)} %filled_hbm.1, bf16[16,128,128]{2,1,0:T(8,128)(2,1)} %fp_hbm.3, ...), custom_call_target="tpu_custom_call" | custom-call | tf_op jit(solution)/shard_map/project_and_exchange/pallas_call | solution.py:576
  23.3 8.8 %back_spread.1 = (bf16[8,8,4096]{2,1,0:T(8,128)(2,1)}, f32[4,8,512]{2,1,0:T(8,128)}) custom-call(s32[24,128]{1,0:T(8,128)} %get-tuple-element.5.table_ref, f32[4,8]{1,0:T(4,128)} %w_ref.3, bf16[16,32,256]{2,1,0:T(8,128)(2,1)} %get-tuple-element.6.sent_hbm, bf16[16,128,128]{2,1,0:T(8,128)(2,1)} %fp_hbm.3, bf16[8,8,4096]{2,1,0:T(8,128)(2,1)} %vol_hbm.3, ...), custom_call_target="tpu_custom_call" | custom-call | tf_op jit(solution)/shard_map/back_spread/pallas_call | solution.py:265
